TPU v7x, 256 devices: a whole 4x4x8 slice. The times are simulated.
256 devices in a mesh: dp: 16 (over x_hi, y, core), tensor: 16 (over z, x_lo).
Axes of the slice: x: 4 (x_hi: 2, x_lo: 2; x = x_hi * 2 + x_lo), y: 4, z: 8, core: 2. Of those that a mesh axis runs over, the one named last changes fastest.
Arguments:
- tokens: bfloat16 [16384, 2560], P(('dp', 'tensor')), may hold values from -6 to 6
- gain: float32 [2560], replicated, may hold values from 0.1 to 1.9
- w_qkv: bfloat16 [3, 2560, 2560], P(None, 'tensor'), may hold values from -3 to 3
- w_out: bfloat16 [2560, 2560], P('tensor'), may hold values from -0.125 to 0.125
- cotangent: bfloat16 [16384, 2560], P(('dp', 'tensor')), may hold values from -6 to 6
Outputs:
- output: bfloat16 [16384, 2560], P(('dp', 'tensor'))
- input_gradient: bfloat16 [16384, 2560], P(('dp', 'tensor'))
- grad_qkv: float32 [3, 2560, 2560], P(None, 'tensor')
- grad_out: float32 [2560, 2560], P('tensor')
All inputs are finite; a program needn't handle non-finite values.
Results may differ from a plain program's by a relative error of at most 0.023.
Values may be sent and summed in bfloat16 or wider, within the bound.
A program may use at most 128 MiB of HBM per device.

v0:
```python
import jax
import jax.numpy as jnp
from jax import lax
from jax.sharding import PartitionSpec as P

HEAD_DIM = 80
LEN = 512


def normalize_rows(x, gain):
    xf = x.astype(jnp.float32)
    row_average = jnp.mean(xf, axis=-1, keepdims=True)
    centered_rows = xf - row_average
    var = jnp.mean(centered_rows * centered_rows, axis=-1, keepdims=True)
    inverse_deviation = lax.rsqrt(var + 1e-05)
    standardized_input = centered_rows * inverse_deviation
    return ((standardized_input * gain).astype(jnp.bfloat16), standardized_input, inverse_deviation)


def split_heads(qkv, heads):
    shaped = qkv.reshape(-1, LEN, 3, heads, HEAD_DIM)
    return (shaped[:, :, 0], shaped[:, :, 1], shaped[:, :, 2])


def attend(query, key, value):
    scale = HEAD_DIM ** (-0.5)
    scores = jnp.einsum("sqhd,skhd->shqk", query, key, preferred_element_type=jnp.float32) * scale
    rows = lax.broadcasted_iota(jnp.int32, (LEN, LEN), 0)
    cols = lax.broadcasted_iota(jnp.int32, (LEN, LEN), 1)
    scores = jnp.where(rows >= cols, scores, -1e30)
    top = jnp.max(scores, axis=-1, keepdims=True)
    expo = jnp.exp(scores - top)
    probs = expo / jnp.sum(expo, axis=-1, keepdims=True)
    probs_low = probs.astype(jnp.bfloat16)
    attended = jnp.einsum(
        "shqk,skhd->sqhd", probs_low, value, preferred_element_type=jnp.float32
    ).astype(jnp.bfloat16)
    return (attended, probs, probs_low)


def attend_back(query, key, value, probs, probs_low, d_att):
    scale = HEAD_DIM ** (-0.5)
    d_value = jnp.einsum("shqk,sqhd->skhd", probs_low, d_att, preferred_element_type=jnp.float32)
    d_probs = jnp.einsum("sqhd,skhd->shqk", d_att, value, preferred_element_type=jnp.float32)
    d_score = probs * (d_probs - jnp.sum(d_probs * probs, axis=-1, keepdims=True)) * scale
    d_low = d_score.astype(jnp.bfloat16)
    d_query = jnp.einsum("shqk,skhd->sqhd", d_low, key, preferred_element_type=jnp.float32)
    d_key = jnp.einsum("shqk,sqhd->skhd", d_low, query, preferred_element_type=jnp.float32)
    return jnp.stack([d_query, d_key, d_value], axis=2).astype(jnp.bfloat16)


def inner_rows(left, right):
    return lax.dot_general(
        left, right, (((0,), (0,)), ((), ())), preferred_element_type=jnp.float32
    )


def inner_cols(left, right):
    return lax.dot_general(
        left, right, (((1,), (1,)), ((), ())), preferred_element_type=jnp.float32
    )


def sum_weights(grad_qkv_part, grad_out_part):
    return (
        lax.psum(grad_qkv_part.astype(jnp.bfloat16), "dp").astype(jnp.float32),
        lax.psum(grad_out_part.astype(jnp.bfloat16), "dp").astype(jnp.float32),
    )


def sum_back(dqkv, flat_w):
    return lax.psum_scatter(
        jnp.dot(dqkv, flat_w, preferred_element_type=jnp.float32).astype(jnp.bfloat16),
        "tensor",
        scatter_dimension=0,
        tiled=True,
    ).astype(jnp.float32)


def per_device(tokens, gain, w_qkv, w_out, cotangent):
    dim = tokens.shape[1]
    width = w_out.shape[0]
    heads = width // HEAD_DIM
    flat_w = w_qkv.reshape(3 * width, dim)
    normalized_rows, standardized_input, inverse_deviation = normalize_rows(tokens, gain)
    qkv = inner_cols(lax.all_gather(normalized_rows, "tensor", axis=0, tiled=True), flat_w).astype(
        jnp.bfloat16
    )
    query, key, value = split_heads(qkv, heads)
    attended, probs, probs_low = attend(query, key, value)
    att_flat = attended.reshape(-1, width)
    mixed = lax.psum_scatter(
        jnp.dot(att_flat, w_out, preferred_element_type=jnp.float32).astype(jnp.bfloat16),
        "tensor",
        scatter_dimension=0,
        tiled=True,
    ).astype(jnp.float32)
    output = (tokens.astype(jnp.float32) + mixed).astype(jnp.bfloat16)
    normed_full, grad_full = (
        lax.all_gather(normalized_rows, "tensor", axis=0, tiled=True),
        lax.all_gather(cotangent, "tensor", axis=0, tiled=True),
    )
    qkv = inner_cols(normed_full, flat_w).astype(jnp.bfloat16)
    query, key, value = split_heads(qkv, heads)
    attended, probs, probs_low = attend(query, key, value)
    att_flat = attended.reshape(-1, width)
    d_att = inner_cols(grad_full, w_out).astype(jnp.bfloat16)
    grad_out_part = inner_rows(att_flat, grad_full)
    d_att = d_att.reshape(-1, LEN, heads, HEAD_DIM)
    dqkv = attend_back(query, key, value, probs, probs_low, d_att).reshape(-1, 3 * width)
    grad_qkv_part = inner_rows(dqkv, normed_full)
    d_norm = sum_back(dqkv, flat_w)
    grad_qkv_sum, grad_out_sum = sum_weights(grad_qkv_part, grad_out_part)
    replicas = lax.axis_size("dp")
    scaled_rows = d_norm * gain
    first_average = jnp.mean(scaled_rows, axis=-1, keepdims=True)
    second_average = jnp.mean(scaled_rows * standardized_input, axis=-1, keepdims=True)
    input_gradient = (
        cotangent.astype(jnp.float32)
        + inverse_deviation * (scaled_rows - first_average - standardized_input * second_average)
    ).astype(jnp.bfloat16)
    grad_qkv = (grad_qkv_sum / replicas).reshape(3, width, dim)
    grad_out = grad_out_sum / replicas
    return (output, input_gradient, grad_qkv, grad_out)


def solution(mesh):
    placed = (
        P(("dp", "tensor"), None),
        P(),
        P(None, "tensor", None),
        P("tensor", None),
        P(("dp", "tensor"), None),
    )
    return jax.shard_map(
        per_device,
        mesh=mesh,
        in_specs=placed,
        out_specs=(
            P(("dp", "tensor"), None),
            P(("dp", "tensor"), None),
            P(None, "tensor", None),
            P("tensor", None),
        ),
        check_vma=False,
    )
```

profile of v0, /device:TPU:1, one launch (start us, length us, event | category | flops | bytes accessed | tf_op | source)
XLA Modules:
  0.0 709.2 jit_solution(3503254380996370441)
XLA Ops:
  7.2 0.0 copy-start
  7.2 0.0 all-gather.3.cloned.1.call-start
  7.2 1.3 convert_reduce_fusion
  8.5 1.2 fusion.37
  9.8 1.9 fusion.31
  11.7 0.0 all-gather.3.cloned.1.call-update
  11.7 0.0 all-gather.5.cloned.1.call-start
  11.8 0.7 all-gather.5.cloned.1.call-update
  12.5 0.0 all-reduce.3.cloned.1.call-start
  12.5 0.8 iota_compare_fusion
  13.3 121.1 %all-gather.3.cloned.1.call-done = bf16[1024,2560]{1,0:T(8,128)(2,1)} async-done(((bf16[64,2560]{1,0:T(8,128)(2,1)}), bf16[1024,2560]{1,0:T(8,128)(2,1)}) %all-gather.3.cloned.1.call-update) | async-done | bytes 5242896 | tf_op jit(solution)/shard_map/all_gather | solution.py:86
  134.4 0.0 copy-done
  134.4 6.2 convolution_convert_fusion.4
  140.6 3.1 reshape.60
  143.7 1.5 fusion.52
  145.2 111.2 %all-gather.5.cloned.1.call-done = bf16[1024,2560]{1,0:T(8,128)(2,1)} async-done(((bf16[64,2560]{1,0:T(8,128)(2,1)}), bf16[1024,2560]{1,0:T(8,128)(2,1)}) %all-gather.5.cloned.1.call-update) | async-done | bytes 5242896 | tf_op jit(solution)/shard_map/all_gather | solution.py:101
  256.4 4.5 convolution_convert_fusion.5
  260.9 0.2 reshape.62
  261.2 0.0 copy-start.4
  261.2 0.0 copy-start.9
  261.2 0.0 copy-done.5
  261.2 2.8 fusion.42
  264.0 0.0 copy-done.9
  264.0 4.8 fusion.53
  268.8 0.0 copy-done.4
  268.8 3.5 fusion.23
  272.3 0.0 copy-done.10
  272.3 8.5 %fusion.17 = bf16[2,512,1,2,80]{1,4,3,0,2:T(8,128)(2,1)} fusion(f32[2,2,512,512]{2,3,1,0:T(8,128)} %fusion.42, bf16[2,512,1,2,80]{1,0,4,3,2:T(2,128)(2,1)S(1)} %copy-done.10, f32[2,2,512,512]{2,3,1,0:T(8,128)} %get-tuple-element.14, f32[2,2,512]{2,1,0:T(2,128)S(1)} %get-tuple-element.13), kind=kOutput, calls=%fused_computation.24 | convolution fusion | flops 175114752 | bytes 9052160 | tf_op jit(solution)/shard_map/shqk,skhd->sqhd/dot_general | solution.py:47
  280.8 8.4 %fusion.20 = bf16[2,512,1,2,80]{1,4,3,0,2:T(8,128)(2,1)} fusion(f32[2,2,512,512]{2,3,1,0:T(8,128)} %fusion.42, bf16[2,512,1,2,80]{1,0,4,3,2:T(2,128)(2,1)} %get-tuple-element.9, f32[2,2,512,512]{2,3,1,0:T(8,128)} %get-tuple-element.14, f32[2,2,512]{2,1,0:T(2,128)S(1)} %get-tuple-element.13), kind=kOutput, calls=%fused_computation.25 | convolution fusion | flops 175114752 | bytes 9052160 | tf_op jit(solution)/shard_map/shqk,sqhd->skhd/dot_general | solution.py:48
  289.3 3.2 convolution_bitcast_fusion
  292.5 0.0 copy-done.8
  292.5 0.3 copy.22
  292.8 0.0 slice-start.2
  292.9 0.0 copy-done.11
  292.9 0.0 copy-done.12
  292.9 0.0 copy-start.2
  292.9 0.1 maximum_convert_fusion
  293.0 1.0 copy.28
  294.1 0.0 slice-start.3
  294.1 0.2 copy.37
  294.3 0.0 copy-start.7
  294.3 0.0 slice-done
  294.3 0.0 slice-done.1
  294.3 2.0 convolution_convert_fusion.3
  296.3 0.0 copy-done.2
  296.3 0.0 copy-done.7
  296.3 0.0 slice-done.2
  296.3 4.0 convolution_convert_fusion.2
  300.3 0.0 all-reduce.3.cloned.1.call-update
  300.3 0.0 reduce-scatter.5.cloned.1.call-start
  300.4 6.2 convolution_convert_fusion.1
  306.5 0.0 reduce-scatter.5.cloned.1.call-update
  306.5 0.0 reduce-scatter.3.cloned.1.call-start
  306.6 0.9 copy-done.3
  307.5 5.1 convolution_convert_fusion
  312.5 0.0 reduce-scatter.3.cloned.1.call-update
  312.6 141.9 %all-reduce.3.cloned.1.call-done = (bf16[480,2560]{1,0:T(8,128)(2,1)}, bf16[160,2560]{1,0:T(8,128)(2,1)}) async-done(((bf16[480,2560]{1,0:T(8,128)(2,1)}, bf16[160,2560]{1,0:T(8,128)(2,1)}), (bf16[480,2560]{1,0:T(8,128)(2,1)}, bf16[160,2560]{1,0:T(8,128)(2,1)})) %all-reduce.3.cloned.1.call-update) | async-done | bytes 3276816 | tf_op jit(solution)/shard_map/psum | solution.py:66
  454.4 2.5 convert_multiply_fusion.1
  456.9 4.7 convert_multiply_fusion
  461.6 116.1 %reduce-scatter.5.cloned.1.call-done = bf16[64,2560]{1,0:T(8,128)(2,1)} async-done(((bf16[1024,2560]{1,0:T(8,128)(2,1)}), bf16[64,2560]{1,0:T(8,128)(2,1)}) %reduce-scatter.5.cloned.1.call-update) | async-done | bytes 327696 | tf_op jit(solution)/shard_map/reduce_scatter | solution.py:72
  577.7 0.0 copy-done.13
  577.7 1.3 fusion.39
  579.1 121.4 %reduce-scatter.3.cloned.1.call-done = bf16[64,2560]{1,0:T(8,128)(2,1)} async-done(((bf16[1024,2560]{1,0:T(8,128)(2,1)}), bf16[64,2560]{1,0:T(8,128)(2,1)}) %reduce-scatter.3.cloned.1.call-update) | async-done | bytes 327696 | tf_op jit(solution)/shard_map/reduce_scatter | solution.py:92
  700.4 2.3 fusion.36
  (20 shorter events, 0.1 us)
Async XLA Ops:
  7.2 127.2 %copy-start = (bf16[3,160,2560]{2,1,0:T(8,128)(2,1)S(1)}, bf16[3,160,2560]{2,1,0:T(8,128)(2,1)}, u32[]{:S(2)}) copy-start(bf16[3,160,2560]{2,1,0:T(8,128)(2,1)} %param.7) | copy-start | bytes 7372804
  7.2 127.2 %all-gather.3.cloned.1.call-start = ((), (), s32[]{:S(2)}) async-start(), calls=%async_computation.2 | async-start | bytes 5570560 | tf_op jit(solution)/shard_map/all_gather | solution.py:86
  11.7 244.7 %all-gather.5.cloned.1.call-start = ((), (), s32[]{:S(2)}) async-start(), calls=%async_computation.4 | async-start | bytes 5570560 | tf_op jit(solution)/shard_map/all_gather | solution.py:101
  12.5 442.0 %all-reduce.3.cloned.1.call-start = ((), (), s32[]{:S(2)}) async-start(), calls=%async_computation.6 | async-start | bytes 6553600 | tf_op jit(solution)/shard_map/psum | solution.py:66
  145.2 116.0 %copy-start.5 = (bf16[2,512,1,2,80]{1,0,4,3,2:T(2,128)(2,1)S(1)}, bf16[2,512,1,2,80]{1,0,4,3,2:T(2,128)(2,1)}, u32[]{:S(2)}) copy-start(bf16[2,512,1,2,80]{1,0,4,3,2:T(2,128)(2,1)} %get-tuple-element.10) | copy-start | bytes 983044
  261.2 7.7 %copy-start.4 = (bf16[2,512,2,80]{1,0,3,2:T(2,128)(2,1)}, bf16[2,512,2,80]{1,0,3,2:T(2,128)(2,1)S(1)}, u32[]{:S(2)}) copy-start(bf16[2,512,2,80]{1,0,3,2:T(2,128)(2,1)S(1)} %reshape.62) | copy-start | bytes 983044
  261.2 2.8 copy-start.9
  268.8 3.5 copy-start.10
  280.8 13.5 %slice-start = ((s8[5242880]{0:T(1024)(128)(4,1)}), s8[1048576]{0:T(1024)(128)(4,1)S(1)}, s32[]{:S(2)}) async-start(s8[5242880]{0:T(1024)(128)(4,1)} %bitcast.72), calls=%async_computation.7 | async-start | bytes 2097152
  289.3 3.2 copy-start.8
  289.3 3.6 copy-start.11
  289.3 3.6 copy-start.12
  289.3 5.1 slice-start.1
  292.8 3.5 slice-start.2
  292.9 3.4 copy-start.2
  294.1 2.3 slice-start.3
  294.3 2.0 copy-start.7
  300.3 277.4 %reduce-scatter.5.cloned.1.call-start = ((), (), s32[]{:S(2)}) async-start(), calls=%async_computation.5 | async-start | bytes 5570560 | tf_op jit(solution)/shard_map/reduce_scatter | solution.py:72
  306.5 1.0 copy-start.3
  306.5 393.9 %reduce-scatter.3.cloned.1.call-start = ((), (), s32[]{:S(2)}) async-start(), calls=%async_computation.3 | async-start | bytes 5570560 | tf_op jit(solution)/shard_map/reduce_scatter | solution.py:92
  456.9 120.8 %copy-start.1 = (bf16[64,2560]{1,0:T(8,128)(2,1)S(1)}, bf16[64,2560]{1,0:T(8,128)(2,1)}, u32[]{:S(2)}) copy-start(bf16[64,2560]{1,0:T(8,128)(2,1)} %param.5) | copy-start | bytes 983044
  456.9 120.8 %copy-start.13 = (f32[2560]{0:T(1024)S(1)}, f32[2560]{0:T(1024)}, u32[]{:S(2)}) copy-start(f32[2560]{0:T(1024)} %param.6) | copy-start | bytes 30724
  456.9 243.5 %copy-start.6 = (bf16[64,2560]{1,0:T(8,128)(2,1)S(1)}, bf16[64,2560]{1,0:T(8,128)(2,1)}, u32[]{:S(2)}) copy-start(bf16[64,2560]{1,0:T(8,128)(2,1)} %param.9) | copy-start | bytes 983044
Sparse Core Ops, SparseCore 0:
  11.8 122.5 all-gather.2
  136.2 120.1 all-gather.4
  300.4 153.9 all-reduce.2
  456.9 120.8 reduce-scatter.4
  580.1 120.2 reduce-scatter.2
where the time goes:
time: 710 us; the launch traced here: 709 us
  waiting for transfers between devices  612 us (86%)
  matrix products  59.1 us (8%)
  other arithmetic  16.1 us (2%)
  between operations  14 us (2%)
  local copies, waits for them, and re-layouts  7.43 us (1%)
    psum x1, waiting for transfers between devices, sum_weights(): lax.psum(grad_qkv_part.astype(jnp.bfloat16), 'dp').astype(jnp.float32)  142 us
    reduce_scatter x1, waiting for transfers between devices, per_device(): lax.psum_scatter(jnp.dot(att_flat, w_out, preferred_element_type=jnp.floa...  121 us
    all_gather x1, waiting for transfers between devices, per_device(): lax.all_gather(normalized_rows, 'tensor', axis=0, tiled=True)  121 us
    reduce_scatter x1, waiting for transfers between devices, sum_back(): lax.psum_scatter(jnp.dot(dqkv, flat_w, preferred_element_type=jnp.float32...  116 us
    all_gather x1, waiting for transfers between devices, per_device(): lax.all_gather(cotangent, 'tensor', axis=0, tiled=True)  111 us
  transfers between devices with their start and end apart: 5, of which 5 were waited for; matrix products, arithmetic and copies ran while one was open for 4% of the time, Pallas kernels for 0%

commit v1 on v0

--- a/solution.py
+++ b/solution.py
@@ -1,10 +1,14 @@
 import jax
 import jax.numpy as jnp
 from jax import lax
+from jax.experimental import pallas as pl
+from jax.experimental.pallas import tpu as pltpu
 from jax.sharding import PartitionSpec as P
 
 HEAD_DIM = 80
 LEN = 512
+MESH = pl.DeviceIdType.MESH
+VMEM_BYTES = 56 * 1024 * 1024
 
 
 def normalize_rows(x, gain):
@@ -61,20 +65,554 @@
     )
 
 
-def sum_weights(grad_qkv_part, grad_out_part):
-    return (
-        lax.psum(grad_qkv_part.astype(jnp.bfloat16), "dp").astype(jnp.float32),
-        lax.psum(grad_out_part.astype(jnp.bfloat16), "dp").astype(jnp.float32),
+class Place:
+    def __init__(self):
+        dp, tensor = lax.axis_index("dp"), lax.axis_index("tensor")
+        self.core = dp % 2
+        self.y = (dp // 2) % 4
+        self.x_lo = tensor % 2
+        self.x = (dp // 8) * 2 + self.x_lo
+        self.z = tensor // 2
+        self.home = self.core == self.x_lo
+        self.away = self.core != self.x_lo
+
+    def at(self, x=None, y=None, z=None, core=None):
+        x = self.x if x is None else x
+        y = self.y if y is None else y
+        z = self.z if z is None else z
+        core = self.core if core is None else core
+        return ((x // 2) * 8 + y * 2 + core, z * 2 + x % 2)
+
+    def pair(self):
+        return self.at(core=1 - self.core)
+
+    def partner(self):
+        return self.at(x=self.x + 1 - 2 * self.x_lo, core=1 - self.core)
+
+    def z_next(self, by):
+        return self.at(z=(self.z + by + 8) % 8)
+
+    def x_next(self, by):
+        return self.at(x=(self.x + by + 4) % 4)
+
+    def y_next(self, by):
+        return self.at(y=(self.y + by + 4) % 4)
+
+
+def greet(devices):
+    barrier = pltpu.get_barrier_semaphore()
+    for device in devices:
+        pl.semaphore_signal(barrier, inc=1, device_id=device, device_id_type=MESH)
+    pl.semaphore_wait(barrier, len(devices))
+
+
+def remote(source, target, send_sem, recv_sem, device):
+    return pltpu.make_async_remote_copy(
+        src_ref=source,
+        dst_ref=target,
+        send_sem=send_sem,
+        recv_sem=recv_sem,
+        device_id=device,
+        device_id_type=MESH,
     )
 
 
-def sum_back(dqkv, flat_w):
-    return lax.psum_scatter(
-        jnp.dot(dqkv, flat_w, preferred_element_type=jnp.float32).astype(jnp.bfloat16),
-        "tensor",
-        scatter_dimension=0,
-        tiled=True,
-    ).astype(jnp.float32)
+def gather_kernel(
+    x_ref,
+    c_ref,
+    wq_ref,
+    wo_ref,
+    x_full,
+    c_full,
+    wq_out,
+    wo_out,
+    local_sem,
+    swap_send,
+    swap_recv,
+    ring_send,
+    ring_recv,
+    pair_send,
+    pair_recv,
+):
+    place = Place()
+    z, core = place.z, place.core
+    rows = x_ref.shape[0]
+    half = rows // 2
+    up, down = place.z_next(1), place.z_next(-1)
+    pair, partner = place.pair(), place.partner()
+    greet([up, down, pair, partner])
+
+    def block(full, owner, side, first=0, count=rows):
+        owner = (owner + 8) % 8
+        start = pl.multiple_of((owner * 2 + side) * rows + first, 32)
+        return full.at[pl.ds(start, count), :]
+
+    fulls = (x_full, c_full)
+    swapped = [
+        (x_ref, block(x_full, z, 1 - core)),
+        (c_ref, block(c_full, z, 1 - core)),
+        (wq_ref, wq_out),
+        (wo_ref, wo_out),
+    ]
+    kept = [
+        (x_ref, block(x_full, z, core)),
+        (c_ref, block(c_full, z, core)),
+        (wq_ref, wq_out),
+        (wo_ref, wo_out),
+    ]
+
+    def swap(i):
+        return remote(*swapped[i], swap_send.at[i], swap_recv.at[i], partner)
+
+    def keep(i):
+        return pltpu.make_async_copy(*kept[i], local_sem.at[i])
+
+    @pl.when(place.away)
+    def _():
+        for i in range(4):
+            swap(i).start()
+
+    @pl.when(place.home)
+    def _():
+        for i in range(4):
+            keep(i).start()
+
+    def settle(i):
+        @pl.when(place.away)
+        def _():
+            swap(i).wait()
+
+        @pl.when(place.home)
+        def _():
+            keep(i).wait()
+
+    def ring(a, way, k):
+        full = fulls[a]
+        owner = z - k if way == 0 else z + k
+        if k < 3:
+            piece = block(full, owner, core)
+        else:
+            piece = block(full, owner, core, 0 if way == 0 else half, half)
+        return remote(
+            piece,
+            piece,
+            ring_send.at[a, way, k],
+            ring_recv.at[a, way, k],
+            up if way == 0 else down,
+        )
+
+    def arrived(a, way, k):
+        full = fulls[a]
+        owner = z - k - 1 if way == 0 else z + k + 1
+        if k < 3:
+            return block(full, owner, core)
+        return block(full, owner, core, 0 if way == 0 else half, half)
+
+    def to_pair(a, i, piece):
+        return remote(piece, piece, pair_send.at[a, i], pair_recv.at[a, i], pair)
+
+    sent = []
+    for a in range(2):
+        settle(a)
+        for way in range(2):
+            ring(a, way, 0).start()
+        copy = to_pair(a, 0, block(fulls[a], z, core))
+        copy.start()
+        sent.append(copy)
+    for k in range(4):
+        for a in range(2):
+            for way in range(2):
+                ring(a, way, k).wait_recv()
+                if k < 3:
+                    ring(a, way, k + 1).start()
+                copy = to_pair(a, 1 + way * 4 + k, arrived(a, way, k))
+                copy.start()
+                sent.append(copy)
+    settle(2)
+    settle(3)
+    for a in range(2):
+        for way in range(2):
+            for k in range(4):
+                ring(a, way, k).wait_send()
+    for copy in sent:
+        copy.wait()
+
+
+def gather_all(normed, cotangent, flat_w, w_out):
+    rows, dim = normed.shape
+    any_space = pl.BlockSpec(memory_space=pl.ANY)
+    dma = pltpu.SemaphoreType.DMA
+    return pl.pallas_call(
+        gather_kernel,
+        out_shape=(
+            jax.ShapeDtypeStruct((rows * 16, dim), jnp.bfloat16),
+            jax.ShapeDtypeStruct((rows * 16, dim), jnp.bfloat16),
+            jax.ShapeDtypeStruct(flat_w.shape, jnp.bfloat16),
+            jax.ShapeDtypeStruct(w_out.shape, jnp.bfloat16),
+        ),
+        in_specs=[any_space] * 4,
+        out_specs=(any_space,) * 4,
+        scratch_shapes=[
+            dma((4,)),
+            dma((4,)),
+            dma((4,)),
+            dma((2, 2, 4)),
+            dma((2, 2, 4)),
+            dma((2, 9)),
+            dma((2, 9)),
+        ],
+        compiler_params=pltpu.CompilerParams(collective_id=0, has_side_effects=True),
+        name="gather_rows",
+    )(normed, cotangent, flat_w, w_out)
+
+
+def sum_into(target, terms):
+    def step(i, carry):
+        here = pl.ds(pl.multiple_of(i * 16, 16), 16)
+        total = terms[0][here, :].astype(jnp.float32)
+        for term in terms[1:]:
+            total = total + term[here, :].astype(jnp.float32)
+        target[here, :] = total.astype(jnp.bfloat16)
+        return carry
+
+    lax.fori_loop(0, target.shape[0] // 16, step, 0)
+
+
+def reduce_kernel(
+    parts_ref,
+    back_ref,
+    g_ref,
+    mixed_out,
+    dnorm_out,
+    g_out,
+    theirs,
+    ring_buf,
+    final,
+    gx_send_buf,
+    gx_buf,
+    gy_src,
+    gy_send_buf,
+    gy_buf,
+    g_work,
+    pair_send,
+    pair_recv,
+    ring_send,
+    ring_recv,
+    swap_send,
+    swap_recv,
+    local_sem,
+    gx_send,
+    gx_recv,
+    gy_send,
+    gy_recv,
+    ga_send,
+    ga_recv,
+    gh_send,
+    gh_recv,
+    gp_send,
+    gp_recv,
+    g_local,
+):
+    place = Place()
+    x, y, z, core = place.x, place.y, place.z, place.core
+    rows = mixed_out.shape[0]
+    dim = mixed_out.shape[1]
+    half = dim // 2
+    up, down = place.z_next(1), place.z_next(-1)
+    pair, partner = place.pair(), place.partner()
+    right, left, across = place.x_next(1), place.x_next(-1), place.x_next(2)
+    north, south = place.y_next(1), place.y_next(-1)
+    greet([up, down, pair, partner, right, left, across, north, south])
+
+    sources = (parts_ref, back_ref)
+    outs = (mixed_out, dnorm_out)
+    wide = (slice(0, half), slice(half, dim))
+    all_columns = slice(0, dim)
+
+    def rows_of(owner, side):
+        owner = (owner + 8) % 8
+        return pl.ds(pl.multiple_of((owner * 2 + side) * rows, 64), rows)
+
+    g_rows = g_ref.shape[0] // 4
+    g_cols = dim // 4
+    g_half = g_rows // 2
+    top, bottom = slice(0, g_half), slice(g_half, g_rows)
+
+    def quarter(q):
+        return pl.ds(pl.multiple_of(((q + 4) % 4) * g_rows, 32), g_rows)
+
+    def columns(q):
+        return pl.ds(pl.multiple_of(((q + 4) % 4) * g_cols, 128), g_cols)
+
+    def gx(way, k):
+        device = right if way == 0 else left
+        if k == 0:
+            return remote(
+                g_ref.at[quarter(x + 2), wide[way]],
+                gx_buf.at[way, 0, :, wide[way]],
+                gx_send.at[way, 0],
+                gx_recv.at[way, 0],
+                device,
+            )
+        return remote(
+            gx_send_buf.at[way],
+            gx_buf.at[way, 1],
+            gx_send.at[way, 1],
+            gx_recv.at[way, 1],
+            device,
+        )
+
+    def gy(way, k):
+        device = north if way == 0 else south
+        part = top if way == 0 else bottom
+        if k == 0:
+            return remote(
+                gy_src.at[part, columns(y + 2)],
+                gy_buf.at[way, 0, part, :],
+                gy_send.at[way, 0],
+                gy_recv.at[way, 0],
+                device,
+            )
+        return remote(
+            gy_send_buf.at[way],
+            gy_buf.at[way, 1],
+            gy_send.at[way, 1],
+            gy_recv.at[way, 1],
+            device,
+        )
+
+    def ga(way, k):
+        device = north if way == 0 else south
+        if k == 0:
+            spot = g_work.at[quarter(x), columns(y)]
+        else:
+            first = 0 if way == 0 else g_half
+            start = pl.multiple_of(x * g_rows + first, 16)
+            spot = g_work.at[pl.ds(start, g_half), columns(y - 1 if way == 0 else y + 1)]
+        return remote(spot, spot, ga_send.at[way, k], ga_recv.at[way, k], device)
+
+    def core_copy(a, j):
+        owner = z + j
+        return remote(
+            sources[a].at[rows_of(owner, 1 - core), :],
+            theirs.at[a, (owner + 8) % 8],
+            pair_send.at[a, j + 3],
+            pair_recv.at[a, j + 3],
+            pair,
+        )
+
+    def ring(a, way, k):
+        sign = 1 if way == 0 else -1
+        owner = (z + sign * (4 - k) + 8) % 8
+        cols = wide[way] if k == 0 else all_columns
+        return remote(
+            theirs.at[a, owner, :, cols],
+            ring_buf.at[a, way, k, :, cols],
+            ring_send.at[a, way, k],
+            ring_recv.at[a, way, k],
+            up if way == 0 else down,
+        )
+
+    for way in range(2):
+        gx(way, 0).start()
+    order = (4, 3, -3, 2, -2, 1, -1, 0)
+    for a in range(2):
+        for j in order:
+            core_copy(a, j).start()
+
+    def sum_step(a, way, k):
+        sign = 1 if way == 0 else -1
+        j = sign * (4 - k)
+        owner = (z + j + 8) % 8
+        own, other = sources[a].at[rows_of(owner, core), :], theirs.at[a, owner]
+        cols, rest = wide[way], wide[1 - way]
+        if k == 0:
+            if way == 0:
+                core_copy(a, 4).wait_recv()
+            sum_into(other.at[:, cols], [own.at[:, cols], other.at[:, cols]])
+        else:
+            core_copy(a, j).wait_recv()
+            ring(a, way, k - 1).wait_recv()
+            came = ring_buf.at[a, way, k - 1]
+            if k == 1:
+                sum_into(other.at[:, cols], [own.at[:, cols], other.at[:, cols], came.at[:, cols]])
+                sum_into(other.at[:, rest], [own.at[:, rest], other.at[:, rest]])
+            else:
+                sum_into(other, [own, other, came])
+        ring(a, way, k).start()
+
+    def z_round(k):
+        for a in range(2):
+            for way in range(2):
+                sum_step(a, way, k)
+
+    z_round(0)
+    for way in range(2):
+        gx(way, 0).wait_recv()
+        own = g_ref.at[quarter(x + 1) if way == 0 else quarter(x - 1), :]
+        target, came = gx_send_buf.at[way], gx_buf.at[way, 0]
+        cols, rest = wide[way], wide[1 - way]
+        sum_into(target.at[:, cols], [own.at[:, cols], came.at[:, cols]])
+        sum_into(target.at[:, rest], [own.at[:, rest]])
+        gx(way, 1).start()
+    z_round(1)
+    z_round(2)
+    for way in range(2):
+        gx(way, 1).wait_recv()
+    sum_into(gy_src, [g_ref.at[quarter(x), :], gx_buf.at[0, 1], gx_buf.at[1, 1]])
+    for way in range(2):
+        gy(way, 0).start()
+    z_round(3)
+    for way in range(2):
+        gy(way, 0).wait_recv()
+        own = gy_src.at[:, columns(y + 1) if way == 0 else columns(y - 1)]
+        target, came = gy_send_buf.at[way], gy_buf.at[way, 0]
+        part, rest = (top, bottom) if way == 0 else (bottom, top)
+        sum_into(target.at[part, :], [own.at[part, :], came.at[part, :]])
+        sum_into(target.at[rest, :], [own.at[rest, :]])
+        gy(way, 1).start()
+    for way in range(2):
+        gy(way, 1).wait_recv()
+    spot = g_work.at[quarter(x), columns(y)]
+    sum_into(spot, [gy_src.at[:, columns(y)], gy_buf.at[0, 1], gy_buf.at[1, 1]])
+    for way in range(2):
+        ga(way, 0).start()
+
+    def swap_back(a):
+        return remote(final.at[a], outs[a], swap_send.at[a], swap_recv.at[a], partner)
+
+    def keep(a):
+        return pltpu.make_async_copy(final.at[a], outs[a], local_sem.at[a])
+
+    for a in range(2):
+        core_copy(a, 0).wait_recv()
+        ring(a, 0, 3).wait_recv()
+        ring(a, 1, 3).wait_recv()
+        own = sources[a].at[rows_of(z, core), :]
+        sum_into(final.at[a], [own, theirs.at[a, z], ring_buf.at[a, 0, 3], ring_buf.at[a, 1, 3]])
+
+        @pl.when(place.away)
+        def _():
+            swap_back(a).start()
+
+        @pl.when(place.home)
+        def _():
+            keep(a).start()
+
+    for way in range(2):
+        ga(way, 0).wait_recv()
+        ga(way, 1).start()
+    for way in range(2):
+        ga(way, 1).wait_recv()
+
+    def to_home(i):
+        spot = g_work.at[quarter(x), :]
+        return remote(spot, spot, gh_send.at[i], gh_recv.at[i], (right, left, across)[i])
+
+    def from_side(i):
+        spot = g_work.at[quarter((x - 1, x + 1, x + 2)[i]), :]
+        return remote(spot, spot, gh_send.at[i], gh_recv.at[i], pair)
+
+    def handed(i):
+        return quarter((x, x - 1, x + 1, x + 2)[i])
+
+    def to_pair(i):
+        source, target = g_work.at[handed(i), :], g_out.at[handed(i), :]
+        return remote(source, target, gp_send.at[i], gp_recv.at[i], pair)
+
+    def to_out(i):
+        return pltpu.make_async_copy(g_work.at[handed(i), :], g_out.at[handed(i), :], g_local.at[i])
+
+    @pl.when(place.away)
+    def _():
+        to_home(0).start()
+        to_home(1).start()
+        for a in range(2):
+            swap_back(a).wait()
+        for i in range(4):
+            to_pair(i).wait_recv()
+        to_home(0).wait_send()
+        to_home(1).wait_send()
+
+    @pl.when(place.home)
+    def _():
+        to_home(2).start()
+        for i in range(4):
+            if i > 0:
+                from_side(i - 1).wait_recv()
+            to_pair(i).start()
+            to_out(i).start()
+        for a in range(2):
+            keep(a).wait()
+        for i in range(4):
+            to_pair(i).wait_send()
+            to_out(i).wait()
+        to_home(2).wait_send()
+
+    for a in range(2):
+        for j in order:
+            core_copy(a, j).wait_send()
+        for way in range(2):
+            for k in range(4):
+                ring(a, way, k).wait_send()
+    for way in range(2):
+        for k in range(2):
+            gx(way, k).wait_send()
+            gy(way, k).wait_send()
+            ga(way, k).wait_send()
+
+
+def reduce_all(parts, back_parts, grads):
+    dim = parts.shape[1]
+    rows = parts.shape[0] // 16
+    g_rows, g_cols = grads.shape[0] // 4, dim // 4
+    vmem = pl.BlockSpec(memory_space=pltpu.VMEM)
+    any_space = pl.BlockSpec(memory_space=pl.ANY)
+    dma = pltpu.SemaphoreType.DMA
+    low = jnp.bfloat16
+    return pl.pallas_call(
+        reduce_kernel,
+        out_shape=(
+            jax.ShapeDtypeStruct((rows, dim), low),
+            jax.ShapeDtypeStruct((rows, dim), low),
+            jax.ShapeDtypeStruct(grads.shape, low),
+        ),
+        in_specs=[vmem] * 3,
+        out_specs=(any_space,) * 3,
+        scratch_shapes=[
+            pltpu.VMEM((2, 8, rows, dim), low),
+            pltpu.VMEM((2, 2, 4, rows, dim), low),
+            pltpu.VMEM((2, rows, dim), low),
+            pltpu.VMEM((2, g_rows, dim), low),
+            pltpu.VMEM((2, 2, g_rows, dim), low),
+            pltpu.VMEM((g_rows, dim), low),
+            pltpu.VMEM((2, g_rows, g_cols), low),
+            pltpu.VMEM((2, 2, g_rows, g_cols), low),
+            pltpu.VMEM(grads.shape, low),
+            dma((2, 8)),
+            dma((2, 8)),
+            dma((2, 2, 4)),
+            dma((2, 2, 4)),
+            dma((2,)),
+            dma((2,)),
+            dma((2,)),
+            dma((2, 2)),
+            dma((2, 2)),
+            dma((2, 2)),
+            dma((2, 2)),
+            dma((2, 2)),
+            dma((2, 2)),
+            dma((3,)),
+            dma((3,)),
+            dma((4,)),
+            dma((4,)),
+            dma((4,)),
+        ],
+        compiler_params=pltpu.CompilerParams(
+            collective_id=1, has_side_effects=True, vmem_limit_bytes=VMEM_BYTES
+        ),
+        name="reduce_parts",
+    )(parts, back_parts, grads)
 
 
 def per_device(tokens, gain, w_qkv, w_out, cotangent):
@@ -83,44 +621,32 @@
     heads = width // HEAD_DIM
     flat_w = w_qkv.reshape(3 * width, dim)
     normalized_rows, standardized_input, inverse_deviation = normalize_rows(tokens, gain)
-    qkv = inner_cols(lax.all_gather(normalized_rows, "tensor", axis=0, tiled=True), flat_w).astype(
-        jnp.bfloat16
-    )
-    query, key, value = split_heads(qkv, heads)
-    attended, probs, probs_low = attend(query, key, value)
-    att_flat = attended.reshape(-1, width)
-    mixed = lax.psum_scatter(
-        jnp.dot(att_flat, w_out, preferred_element_type=jnp.float32).astype(jnp.bfloat16),
-        "tensor",
-        scatter_dimension=0,
-        tiled=True,
-    ).astype(jnp.float32)
-    output = (tokens.astype(jnp.float32) + mixed).astype(jnp.bfloat16)
-    normed_full, grad_full = (
-        lax.all_gather(normalized_rows, "tensor", axis=0, tiled=True),
-        lax.all_gather(cotangent, "tensor", axis=0, tiled=True),
-    )
+    normed_full, grad_full, flat_w, w_out = gather_all(normalized_rows, cotangent, flat_w, w_out)
     qkv = inner_cols(normed_full, flat_w).astype(jnp.bfloat16)
     query, key, value = split_heads(qkv, heads)
     attended, probs, probs_low = attend(query, key, value)
     att_flat = attended.reshape(-1, width)
+    parts = jnp.dot(att_flat, w_out, preferred_element_type=jnp.float32).astype(jnp.bfloat16)
     d_att = inner_cols(grad_full, w_out).astype(jnp.bfloat16)
-    grad_out_part = inner_rows(att_flat, grad_full)
+    grad_out_part = inner_rows(att_flat, grad_full).astype(jnp.bfloat16)
     d_att = d_att.reshape(-1, LEN, heads, HEAD_DIM)
     dqkv = attend_back(query, key, value, probs, probs_low, d_att).reshape(-1, 3 * width)
-    grad_qkv_part = inner_rows(dqkv, normed_full)
-    d_norm = sum_back(dqkv, flat_w)
-    grad_qkv_sum, grad_out_sum = sum_weights(grad_qkv_part, grad_out_part)
+    grad_qkv_part = inner_rows(dqkv, normed_full).astype(jnp.bfloat16)
+    back_parts = jnp.dot(dqkv, flat_w, preferred_element_type=jnp.float32).astype(jnp.bfloat16)
+    grads = jnp.concatenate([grad_qkv_part, grad_out_part], axis=0)
+    mixed, d_norm, grad_sums = reduce_all(parts, back_parts, grads)
+    output = (tokens.astype(jnp.float32) + mixed.astype(jnp.float32)).astype(jnp.bfloat16)
     replicas = lax.axis_size("dp")
-    scaled_rows = d_norm * gain
+    scaled_rows = d_norm.astype(jnp.float32) * gain
     first_average = jnp.mean(scaled_rows, axis=-1, keepdims=True)
     second_average = jnp.mean(scaled_rows * standardized_input, axis=-1, keepdims=True)
     input_gradient = (
         cotangent.astype(jnp.float32)
         + inverse_deviation * (scaled_rows - first_average - standardized_input * second_average)
     ).astype(jnp.bfloat16)
-    grad_qkv = (grad_qkv_sum / replicas).reshape(3, width, dim)
-    grad_out = grad_out_sum / replicas
+    grad_sums = grad_sums.astype(jnp.float32) / replicas
+    grad_qkv = grad_sums[: 3 * width].reshape(3, width, dim)
+    grad_out = grad_sums[3 * width :]
     return (output, input_gradient, grad_qkv, grad_out)
 
 

time: 710 us -> 297 us (0.42)
  waiting for transfers between devices: 612 us -> 0 us
  Pallas kernels: 0 us -> 223 us
  between operations: 14 us -> 0.84 us
  matrix products: 59.1 us -> 51.1 us
    reduce_scatter x2 -> x0, waiting for transfers between devices: 237 us -> none  [the longest x1 121 us: per_device(): lax.psum_scatter(jnp.dot(att_flat, w_out, preferred_element_type=jnp.floa...]
    all_gather x2 -> x0, waiting for transfers between devices: 232 us -> none  [the longest x1 121 us: per_device(): lax.all_gather(normalized_rows, 'tensor', axis=0, tiled=True)]
    pallas_call x0 -> x2, Pallas kernels: none -> 223 us  [the longest x1 154 us: reduce_all(): pl.pallas_call(reduce_kernel, out_shape=(jax.ShapeDtypeStruct((rows, dim)...]
    psum x1 -> x0, waiting for transfers between devices: 142 us -> none  [sum_weights(): lax.psum(grad_qkv_part.astype(jnp.bfloat16), 'dp').astype(jnp.float32)]
  transfers between devices with their start and end apart: 5 -> 0, of which waited for: 5 -> 0; matrix products, arithmetic and copies ran while one was open for 4% -> 0% of each run, Pallas kernels for 0% -> 0%
where the time goes in v1:
time: 297 us
  Pallas kernels  223 us (75%)
  matrix products  51.1 us (17%)
  other arithmetic  12.8 us (4%)
  local copies, waits for them, and re-layouts  9.75 us (3%)
    pallas_call x1, Pallas kernels, reduce_all(): pl.pallas_call(reduce_kernel, out_shape=(jax.ShapeDtypeStruct((rows, dim)...  154 us
    pallas_call x1, Pallas kernels, gather_all(): pl.pallas_call(gather_kernel, out_shape=(jax.ShapeDtypeStruct((rows * 16,...  68.7 us
    dot_general x2, matrix products, inner_cols(): lax.dot_general(left, right, (((1,), (1,)), ((), ())), preferred_element_...  10.5 us
    dot_general x1, matrix products, attend_back(): jnp.einsum('shqk,skhd->sqhd', d_low, key, preferred_element_type=jnp.floa...  7.69 us
    dot_general x1, matrix products, attend_back(): jnp.einsum('shqk,sqhd->skhd', d_low, query, preferred_element_type=jnp.fl...  7.63 us
    dot_general x2, matrix products, inner_rows(): lax.dot_general(left, right, (((0,), (0,)), ((), ())), preferred_element_...  6.46 us

profile of v1, /device:TPU:1, one launch (start us, length us, event | category | flops | bytes accessed | tf_op | source)
XLA Modules:
  0.0 297.1 jit_solution(8084413283607162688)
XLA Ops:
  0.6 1.1 convert_reduce_fusion
  1.8 1.2 fusion.44
  3.0 0.1 iota_compare_fusion
  3.1 1.9 fusion.38.x_ref
  5.0 68.7 %gather_rows.1 = (bf16[1024,2560]{1,0:T(8,128)(2,1)}, bf16[1024,2560]{1,0:T(8,128)(2,1)}, bf16[480,2560]{1,0:T(8,128)(2,1)}, bf16[160,2560]{1,0:T(8,128)(2,1)}) custom-call(bf16[64,2560]{1,0:T(8,128)(2,1)} %fusion.38.x_ref, bf16[64,2560]{1,0:T(8,128)(2,1)} %c_ref.1, bf16[480,2560]{1,0:T(8,128)(2,1)} %bitcast.76, bf16[160,2560]{1,0:T(8,128)(2,1)} %wo_ref.1), custom_call_target="tpu_custom_call" | custom-call | tf_op jit(solution)/shard_map/gather_rows/pallas_call | solution.py:245
  73.7 4.5 %convolution_convert_fusion.6 = bf16[1024,160]{0,1:T(8,128)(2,1)S(1)} fusion(bf16[1024,2560]{1,0:T(8,128)(2,1)} %get-tuple-element.14, bf16[160,2560]{1,0:T(8,128)(2,1)} %get-tuple-element.13), kind=kOutput, calls=%fused_computation.26 | convolution fusion | flops 839024640 | bytes 6389760 | tf_op jit(solution)/shard_map/dot_general | solution.py:63
  78.2 0.2 reshape.53
  78.5 6.0 %convolution_convert_fusion.4 = bf16[1024,480]{0,1:T(8,128)(2,1)S(1)} fusion(bf16[1024,2560]{1,0:T(8,128)(2,1)} %get-tuple-element.11, bf16[480,2560]{1,0:T(8,128)(2,1)} %get-tuple-element.12), kind=kOutput, calls=%fused_computation.22 | convolution fusion | flops 2517073920 | bytes 8683520 | tf_op jit(solution)/shard_map/dot_general | solution.py:63
  84.5 0.7 reshape.51
  85.2 0.7 fusion.59
  85.9 3.7 %fusion.60 = (f32[2,2,512]{2,1,0:T(2,128)S(1)}, f32[2,2,512,512]{2,3,1,0:T(8,128)}) fusion(pred[512,512]{0,1:T(8,128)(4,1)S(1)} %iota_compare_fusion, bf16[2,512,1,2,80]{1,0,4,3,2:T(2,128)(2,1)S(1)} %get-tuple-element.21, bf16[2,512,1,2,80]{1,0,4,3,2:T(2,128)(2,1)S(1)} %get-tuple-element.20), kind=kOutput, calls=%fused_computation.73 | convolution fusion | flops 171966976 | bytes 5120000 | tf_op jit(solution)/shard_map/sub | solution.py:36
  89.6 0.0 copy-start.5
  89.6 0.0 slice-start
  89.6 3.1 %fusion.24 = bf16[2,512,1,2,80]{1,4,3,0,2:T(8,128)(2,1)S(1)} fusion(bf16[2,512,2,80]{1,0,3,2:T(2,128)(2,1)S(1)} %reshape.53, f32[2,2,512,512]{2,3,1,0:T(8,128)} %get-tuple-element.26, f32[2,2,512]{2,1,0:T(2,128)S(1)} %get-tuple-element.25), kind=kOutput, calls=%fused_computation.29 | convolution fusion | flops 170033152 | bytes 4857856 | tf_op jit(solution)/shard_map/shqk,sqhd->skhd/dot_general | solution.py:47
  92.7 0.3 copy-done.5
  93.1 0.0 slice-start.1
  93.1 0.5 fusion.23
  93.6 0.3 copy.22
  93.9 0.0 slice-done
  94.0 1.4 slice-done.1
  95.3 1.1 convolution_convert_fusion.3
  96.4 2.8 fusion.49
  99.1 7.7 %fusion.28 = bf16[2,512,1,2,80]{1,4,3,0,2:T(8,128)(2,1)S(1)} fusion(f32[2,2,512,512]{2,3,1,0:T(8,128)} %fusion.49, bf16[2,512,1,2,80]{1,0,4,3,2:T(2,128)(2,1)S(1)} %get-tuple-element.20, f32[2,2,512,512]{2,3,1,0:T(8,128)} %get-tuple-element.26, f32[2,2,512]{2,1,0:T(2,128)S(1)} %get-tuple-element.25), kind=kOutput, calls=%fused_computation.31 | convolution fusion | flops 175278592 | bytes 9052160 | tf_op jit(solution)/shard_map/shqk,skhd->sqhd/dot_general | solution.py:51
  106.8 7.6 %fusion.25 = bf16[2,512,1,2,80]{1,4,3,0,2:T(8,128)(2,1)S(1)} fusion(f32[2,2,512,512]{2,3,1,0:T(8,128)} %fusion.49, bf16[2,512,1,2,80]{1,0,4,3,2:T(2,128)(2,1)S(1)} %get-tuple-element.21, f32[2,2,512,512]{2,3,1,0:T(8,128)} %get-tuple-element.26, f32[2,2,512]{2,1,0:T(2,128)S(1)} %get-tuple-element.25), kind=kOutput, calls=%fused_computation.30 | convolution fusion | flops 175278592 | bytes 9052160 | tf_op jit(solution)/shard_map/shqk,sqhd->skhd/dot_general | solution.py:52
  114.5 0.1 pad_maximum_fusion.1
  114.6 1.0 copy.28
  115.6 0.2 copy.37
  115.8 5.4 %convolution_convert_fusion.2 = bf16[480,2560]{1,0:T(8,128)(2,1)S(1)} fusion(bf16[1024,480]{0,1:T(8,128)(2,1)S(1)} %bitcast.78, bf16[1024,2560]{1,0:T(8,128)(2,1)} %get-tuple-element.11), kind=kOutput, calls=%fused_computation.5 | convolution fusion | flops 2517811200 | bytes 8683520 | tf_op jit(solution)/shard_map/dot_general | solution.py:57
  121.3 0.0 copy-start.4
  121.3 1.9 pad_maximum_fusion.g_ref
  123.2 0.9 copy-done.4
  124.1 0.0 copy-start.2
  124.1 4.7 %convolution_convert_fusion.1.back_ref = bf16[1024,2560]{1,0:T(8,128)(2,1)} fusion(bf16[1024,480]{0,1:T(8,128)(2,1)S(1)} %bitcast.79, bf16[480,2560]{1,0:T(8,128)(2,1)S(1)} %copy-done.4), kind=kOutput, calls=%fused_computation.4 | convolution fusion | flops 2519203840 | bytes 8683520 | tf_op jit(solution)/shard_map/dot_general | solution.py:635
  128.9 0.0 copy-done.2
  128.9 3.9 %convolution_convert_fusion.parts_ref = bf16[1024,2560]{1,0:T(8,128)(2,1)} fusion(bf16[1024,160]{0,1:T(8,128)(2,1)S(1)} %bitcast.74, bf16[160,2560]{1,0:T(8,128)(2,1)S(1)} %copy-done.2), kind=kOutput, calls=%fused_computation.3 | convolution fusion | flops 841482240 | bytes 6389760 | tf_op jit(solution)/shard_map/dot_general | solution.py:629
  132.8 0.0 copy-start
  132.8 0.0 copy-start.3
  132.8 0.0 copy-start.1
  132.8 154.0 %reduce_parts.1 = (bf16[64,2560]{1,0:T(8,128)(2,1)}, bf16[64,2560]{1,0:T(8,128)(2,1)}, bf16[640,2560]{1,0:T(8,128)(2,1)}) custom-call(bf16[1024,2560]{1,0:T(8,128)(2,1)} %convolution_convert_fusion.parts_ref, bf16[1024,2560]{1,0:T(8,128)(2,1)} %convolution_convert_fusion.1.back_ref, bf16[640,2560]{1,0:T(8,128)(2,1)} %pad_maximum_fusion.g_ref), custom_call_target="tpu_custom_call" | custom-call | tf_op jit(solution)/shard_map/reduce_parts/pallas_call | solution.py:573
  286.8 0.0 copy-done
  286.8 0.0 copy-done.3
  286.8 1.3 fusion.46
  288.2 0.0 copy-done.1
  288.2 2.3 fusion.43
  290.5 2.8 convert_multiply_fusion
  293.3 1.3 slice.24
  294.5 2.6 slice.23
  (5 shorter events, 0.1 us)
Async XLA Ops:
  89.6 3.4 %copy-start.5 = (f32[2,2,512,512]{2,3,1,0:T(8,128)S(1)}, f32[2,2,512,512]{2,3,1,0:T(8,128)}, u32[]{:S(2)}) copy-start(f32[2,2,512,512]{2,3,1,0:T(8,128)} %get-tuple-element.26) | copy-start | bytes 12582916
  89.6 4.3 %slice-start = ((s8[5242880]{0:T(1024)(128)(4,1)}), s8[1048576]{0:T(1024)(128)(4,1)S(1)}, s32[]{:S(2)}) async-start(s8[5242880]{0:T(1024)(128)(4,1)} %bitcast.70), calls=%async_computation | async-start | bytes 2097152
  93.1 2.3 slice-start.1
  121.3 2.9 copy-start.4
  124.1 4.7 %copy-start.2 = (bf16[160,2560]{1,0:T(8,128)(2,1)S(1)}, bf16[160,2560]{1,0:T(8,128)(2,1)}, u32[]{:S(2)}) copy-start(bf16[160,2560]{1,0:T(8,128)(2,1)} %get-tuple-element.13) | copy-start | bytes 2457604
  132.8 154.0 %copy-start = (bf16[64,2560]{1,0:T(8,128)(2,1)S(1)}, bf16[64,2560]{1,0:T(8,128)(2,1)}, u32[]{:S(2)}) copy-start(bf16[64,2560]{1,0:T(8,128)(2,1)} %param.5) | copy-start | bytes 983044
  132.8 154.0 %copy-start.3 = (f32[2560]{0:T(1024)S(1)}, f32[2560]{0:T(1024)}, u32[]{:S(2)}) copy-start(f32[2560]{0:T(1024)} %param.6) | copy-start | bytes 30724
  132.8 155.4 %copy-start.1 = (bf16[64,2560]{1,0:T(8,128)(2,1)S(1)}, bf16[64,2560]{1,0:T(8,128)(2,1)}, u32[]{:S(2)}) copy-start(bf16[64,2560]{1,0:T(8,128)(2,1)} %c_ref.1) | copy-start | bytes 983044

commit v2 on v0

v2 whole, which is shorter than its diff:
```python
import jax
import jax.numpy as jnp
from jax import lax
from jax.experimental import pallas as pl
from jax.experimental.pallas import tpu as pltpu
from jax.sharding import PartitionSpec as P

HEAD_DIM = 80
LEN = 512
PAD = 128
BLOCK = 64
SCALE = HEAD_DIM ** (-0.5)
MESH = pl.DeviceIdType.MESH
VMEM_BYTES = 60 * 1024 * 1024
LOW = jnp.bfloat16
WIDE = jnp.float32


class Place:
    def __init__(self):
        dp, tensor = lax.axis_index("dp"), lax.axis_index("tensor")
        self.core = dp % 2
        self.y = (dp // 2) % 4
        self.x_lo = tensor % 2
        self.x = (dp // 8) * 2 + self.x_lo
        self.z = tensor // 2
        self.home = self.core == self.x_lo
        self.away = self.core != self.x_lo

    def at(self, x=None, y=None, z=None, core=None):
        x = self.x if x is None else x
        y = self.y if y is None else y
        z = self.z if z is None else z
        core = self.core if core is None else core
        return ((x // 2) * 8 + y * 2 + core, z * 2 + x % 2)

    def pair(self):
        return self.at(core=1 - self.core)

    def crossed(self, by):
        return self.at(x=(self.x + by + 4) % 4, core=1 - self.core)

    def partner(self):
        return self.crossed(1 - 2 * self.x_lo)

    def z_next(self, by):
        return self.at(z=(self.z + by + 8) % 8)

    def x_next(self, by):
        return self.at(x=(self.x + by + 4) % 4)

    def y_next(self, by):
        return self.at(y=(self.y + by + 4) % 4)


def greet(devices):
    barrier = pltpu.get_barrier_semaphore()
    for device in devices:
        pl.semaphore_signal(barrier, inc=1, device_id=device, device_id_type=MESH)
    pl.semaphore_wait(barrier, len(devices))


def remote(source, target, send_sem, recv_sem, device):
    return pltpu.make_async_remote_copy(
        src_ref=source,
        dst_ref=target,
        send_sem=send_sem,
        recv_sem=recv_sem,
        device_id=device,
        device_id_type=MESH,
    )


def sum_into(target, terms):
    def step(i, carry):
        here = pl.ds(pl.multiple_of(i * 16, 16), 16)
        total = terms[0][here, :].astype(jnp.float32)
        for term in terms[1:]:
            total = total + term[here, :].astype(jnp.float32)
        target[here, :] = total.astype(jnp.bfloat16)
        return carry

    lax.fori_loop(0, target.shape[0] // 16, step, 0)


def nt(left, right):
    return lax.dot_general(left, right, (((1,), (1,)), ((), ())), preferred_element_type=WIDE)


def tn(left, right):
    return lax.dot_general(left, right, (((0,), (0,)), ((), ())), preferred_element_type=WIDE)


def nn(left, right):
    return jnp.dot(left, right, preferred_element_type=WIDE)


def standardize(x):
    xf = x.astype(WIDE)
    centered = xf - jnp.mean(xf, axis=-1, keepdims=True)
    var = jnp.mean(centered * centered, axis=-1, keepdims=True)
    rstd = lax.rsqrt(var + 1e-05)
    return centered * rstd, rstd


def loop(count, body):
    def step(i, carry):
        body(i)
        return carry

    lax.fori_loop(0, count, step, 0)


def layer_kernel(
    tokens,
    gain,
    wq_ref,
    wo_ref,
    cot,
    out_ref,
    ingrad_ref,
    g_out,
    stage,
    x_full,
    c_full,
    wq,
    wo,
    qkv,
    att,
    datt,
    dqkv,
    probs,
    dk_sum,
    dv_sum,
    parts,
    backs,
    theirs,
    first_buf,
    ring_buf,
    final,
    landed,
    g,
    f_first,
    f_buf,
    e_sum,
    s_first,
    s_buf,
    g_work,
    local_sem,
    swap_send,
    swap_recv,
    w_local,
    w_send,
    w_recv,
    gr_send,
    gr_recv,
    gp_send,
    gp_recv,
    core_send,
    core_recv,
    ring_send,
    ring_recv,
    back_send,
    back_recv,
    back_local,
    f_send,
    f_recv,
    s_send,
    s_recv,
    ga_send,
    ga_recv,
    gh_send,
    gh_recv,
    go_send,
    go_recv,
    go_local,
):
    place = Place()
    x, y, z, core = place.x, place.y, place.z, place.core
    dim = tokens.shape[1]
    rows = BLOCK
    half = rows // 2
    mid = dim // 2
    up, down = place.z_next(1), place.z_next(-1)
    pair, partner = place.pair(), place.partner()
    right, left, across = place.x_next(1), place.x_next(-1), place.x_next(2)
    north, south = place.y_next(1), place.y_next(-1)
    cross_right, cross_left = place.crossed(1), place.crossed(-1)

    for i in range(6):
        wq[i * PAD + HEAD_DIM : (i + 1) * PAD, :] = jnp.zeros((PAD - HEAD_DIM, dim), LOW)
    for i in range(2):
        wo[i * PAD + HEAD_DIM : (i + 1) * PAD, :] = jnp.zeros((PAD - HEAD_DIM, dim), LOW)

    def norm_rows(i):
        here = pl.ds(pl.multiple_of(i * 16, 16), 16)
        xhat, _ = standardize(tokens[here, :])
        stage[here, :] = (xhat * gain[...]).astype(LOW)

    loop(rows // 16, norm_rows)
    greet([up, down, pair, cross_right, cross_left, right, left, across, north, south])

    def block(full, owner, side, first=0, count=rows):
        owner = (owner + 8) % 8
        start = pl.multiple_of((owner * 2 + side) * rows + first, 32)
        return full.at[pl.ds(start, count), :]

    fulls, owned = (x_full, c_full), (stage, cot)

    def swap(a):
        target = block(fulls[a], z, 1 - core)
        return remote(owned[a], target, swap_send.at[a], swap_recv.at[a], partner)

    def keep(a):
        return pltpu.make_async_copy(owned[a], block(fulls[a], z, core), local_sem.at[a])

    def weight_ends(i, h):
        if i < 3:
            source = wq_ref.at[i, pl.ds(h * HEAD_DIM, HEAD_DIM), :]
            return source, wq.at[pl.ds((2 * i + h) * PAD, HEAD_DIM), :]
        return wo_ref.at[pl.ds(h * HEAD_DIM, HEAD_DIM), :], wo.at[pl.ds(h * PAD, HEAD_DIM), :]

    def weight_swap(i, h):
        device = cross_right if h == 0 else cross_left
        return remote(*weight_ends(i, h), w_send.at[i, h], w_recv.at[i, h], device)

    def weight_keep(i, h):
        return pltpu.make_async_copy(*weight_ends(i, h), w_local.at[i, h])

    weights = [(i, h) for i in range(4) for h in range(2)]

    @pl.when(place.away)
    def _():
        for a in range(2):
            swap(a).start()
        for i, h in weights:
            weight_swap(i, h).start()

    @pl.when(place.home)
    def _():
        for a in range(2):
            keep(a).start()
        for i, h in weights:
            weight_keep(i, h).start()

    def settle(a):
        @pl.when(place.away)
        def _():
            swap(a).wait_recv()

        @pl.when(place.home)
        def _():
            keep(a).wait()

    def gather_piece(a, way, k, hops):
        owner = z - hops if way == 0 else z + hops
        if k < 3:
            return block(fulls[a], owner, core)
        return block(fulls[a], owner, core, 0 if way == 0 else half, half)

    def gather(a, way, k):
        piece = gather_piece(a, way, k, k)
        device = up if way == 0 else down
        return remote(piece, piece, gr_send.at[a, way, k], gr_recv.at[a, way, k], device)

    def to_pair(a, i):
        if i == 0:
            piece = block(fulls[a], z, core)
        else:
            way, k = (i - 1) // 4, (i - 1) % 4
            piece = gather_piece(a, way, k, k + 1)
        return remote(piece, piece, gp_send.at[a, i], gp_recv.at[a, i], pair)

    def begin(a):
        settle(a)
        for way in range(2):
            gather(a, way, 0).start()
        to_pair(a, 0).start()

    def advance(a, k):
        for way in range(2):
            gather(a, way, k).wait_recv()
            if k < 3:
                gather(a, way, k + 1).start()
            to_pair(a, 1 + way * 4 + k).start()

    def gathered(a):
        for i in range(9):
            to_pair(a, i).wait_recv()

    begin(0)
    for k in range(3):
        advance(0, k)
    begin(1)
    advance(0, 3)

    @pl.when(place.away)
    def _():
        for i, h in weights:
            weight_swap(i, h).wait_recv()

    @pl.when(place.home)
    def _():
        for i, h in weights:
            weight_keep(i, h).wait()

    gathered(0)

    def project(j):
        here = pl.ds(pl.multiple_of(j * 256, 256), 256)
        for i in range(3):
            cols = slice(i * 256, (i + 1) * 256)
            qkv[here, cols] = nt(x_full[here, :], wq[cols, :]).astype(LOW)

    def spots(u):
        r0 = pl.multiple_of((u // 2) * LEN, LEN)
        c0 = pl.multiple_of((u % 2) * PAD, PAD)
        return r0, c0

    def forward(u):
        r0, c0 = spots(u)
        for i in range(4):
            n = (i + 1) * 128
            here = pl.ds(r0 + i * 128, 128)
            query = qkv[here, pl.ds(c0, PAD)]
            key = qkv[pl.ds(r0, n), pl.ds(c0 + 256, PAD)]
            value = qkv[pl.ds(r0, n), pl.ds(c0 + 512, PAD)]
            scores = nt(query, key) * SCALE
            q_at = lax.broadcasted_iota(jnp.int32, (128, n), 0) + i * 128
            k_at = lax.broadcasted_iota(jnp.int32, (128, n), 1)
            scores = jnp.where(q_at >= k_at, scores, -1e30)
            expo = jnp.exp(scores - jnp.max(scores, axis=-1, keepdims=True))
            p = expo * (1.0 / jnp.sum(expo, axis=-1, keepdims=True))
            probs[u, i * 128 : (i + 1) * 128, :n] = p
            att[here, pl.ds(c0, PAD)] = nn(p.astype(LOW), value).astype(LOW)

    def two(first, body):
        loop(2, lambda i: body(first + i))

    two(0, project)
    advance(1, 0)
    two(2, project)
    two(0, forward)
    advance(1, 1)
    two(2, forward)

    def out_parts(j):
        here = pl.ds(pl.multiple_of(j * 256, 256), 256)
        for i in range(10):
            cols = slice(i * 256, (i + 1) * 256)
            parts[here, cols] = nn(att[here, :], wo[:, cols]).astype(LOW)

    loop(4, out_parts)

    sources = (parts, backs)
    wide = (slice(0, mid), slice(mid, dim))
    order = (4, 3, -3, 2, -2, 1, -1, 0)

    def core_copy(a, j):
        owner = (z + j + 8) % 8
        source = block(sources[a], owner, 1 - core)
        return remote(
            source, theirs.at[a, owner], core_send.at[a, j + 3], core_recv.at[a, j + 3], pair
        )

    def ring(a, way, k):
        sign = 1 if way == 0 else -1
        owner = (z + sign * (4 - k) + 8) % 8
        if k == 0:
            source, target = theirs.at[a, owner, :, wide[way]], first_buf.at[a, :, wide[way]]
        else:
            source, target = theirs.at[a, owner], ring_buf.at[a, way, k - 1]
        device = up if way == 0 else down
        return remote(source, target, ring_send.at[a, way, k], ring_recv.at[a, way, k], device)

    def sum_step(a, way, k):
        sign = 1 if way == 0 else -1
        j = sign * (4 - k)
        owner = (z + j + 8) % 8
        own, other = block(sources[a], owner, core), theirs.at[a, owner]
        cols, rest = wide[way], wide[1 - way]
        if k == 0:
            if way == 0:
                core_copy(a, 4).wait_recv()
            sum_into(other.at[:, cols], [own.at[:, cols], other.at[:, cols]])
        else:
            core_copy(a, j).wait_recv()
            ring(a, way, k - 1).wait_recv()
            if k == 1:
                came = first_buf.at[a, :, cols]
                sum_into(other.at[:, cols], [own.at[:, cols], other.at[:, cols], came])
                sum_into(other.at[:, rest], [own.at[:, rest], other.at[:, rest]])
            else:
                sum_into(other, [own, other, ring_buf.at[a, way, k - 2]])
        ring(a, way, k).start()

    def z_round(a, k):
        for way in range(2):
            sum_step(a, way, k)

    def swap_back(a):
        return remote(final.at[a], landed.at[a], back_send.at[a], back_recv.at[a], partner)

    def keep_back(a):
        return pltpu.make_async_copy(final.at[a], landed.at[a], back_local.at[a])

    def z_final(a):
        core_copy(a, 0).wait_recv()
        ring(a, 0, 3).wait_recv()
        ring(a, 1, 3).wait_recv()
        own = block(sources[a], z, core)
        came = [ring_buf.at[a, 0, 2], ring_buf.at[a, 1, 2]]
        sum_into(final.at[a], [own, theirs.at[a, z]] + came)

        @pl.when(place.away)
        def _():
            swap_back(a).start()

        @pl.when(place.home)
        def _():
            keep_back(a).start()

    for j in order:
        core_copy(0, j).start()
    advance(1, 2)
    z_round(0, 0)
    advance(1, 3)
    gathered(1)

    def project_back(j):
        here = pl.ds(pl.multiple_of(j * 256, 256), 256)
        datt[here, :] = nt(c_full[here, :], wo[...]).astype(LOW)

    def backward(u):
        r0, c0 = spots(u)
        for i in (3, 2, 1, 0):
            n = (i + 1) * 128
            here = pl.ds(r0 + i * 128, 128)
            query = qkv[here, pl.ds(c0, PAD)]
            key = qkv[pl.ds(r0, n), pl.ds(c0 + 256, PAD)]
            value = qkv[pl.ds(r0, n), pl.ds(c0 + 512, PAD)]
            d_att = datt[here, pl.ds(c0, PAD)]
            p = probs[u, i * 128 : (i + 1) * 128, :n]
            d_probs = nt(d_att, value)
            d_score = p * (d_probs - jnp.sum(d_probs * p, axis=-1, keepdims=True)) * SCALE
            d_low = d_score.astype(LOW)
            dqkv[here, pl.ds(c0, PAD)] = nn(d_low, key).astype(LOW)
            dk, dv = tn(d_low, query), tn(p.astype(LOW), d_att)
            if i == 3:
                dk_sum[...] = dk
                dv_sum[...] = dv
            else:
                dk_sum[:n, :] += dk
                dv_sum[:n, :] += dv
        dqkv[pl.ds(r0, LEN), pl.ds(c0 + 256, PAD)] = dk_sum[...].astype(LOW)
        dqkv[pl.ds(r0, LEN), pl.ds(c0 + 512, PAD)] = dv_sum[...].astype(LOW)

    loop(4, project_back)
    z_round(0, 1)
    two(0, backward)
    two(2, backward)
    z_round(0, 2)

    for j in range(4):
        lanes = slice(j * 256, (j + 1) * 256)
        for i in range(3):
            backs[i * 256 : (i + 1) * 256, lanes] = dqkv[lanes, i * 256 : (i + 1) * 256].T
        backs[768:1024, lanes] = att[lanes, :].T

    def weight_grads(j):
        cols = pl.ds(pl.multiple_of(j * 256, 256), 256)
        for i in range(4):
            factor = backs[i * 256 : (i + 1) * 256, 0:1024]
            total = nn(factor, (x_full if i < 3 else c_full)[:, cols]).astype(LOW)
            for h in range(2):
                spot = i * 160 + h * HEAD_DIM
                g[spot : spot + HEAD_DIM, cols] = total[h * PAD : h * PAD + HEAD_DIM, :]

    loop(10, weight_grads)

    side_rows, sub, width = 320, 80, dim // 4
    firsts, seconds = (x, y), (y, x)
    neighbours = ((right, left), (north, south))
    top, bottom = slice(0, 160), slice(160, 320)
    sub_top, sub_bottom = slice(0, 48), slice(48, 80)

    def columns(q):
        return pl.ds(pl.multiple_of(((q + 4) % 4) * width, 128), width)

    def g_side(s, q):
        return g.at[pl.ds(s * side_rows, side_rows), columns(q)]

    def sub_rows(q):
        return pl.ds(pl.multiple_of(((q + 4) % 4) * sub, 16), sub)

    def f_copy(s, way, k):
        device = neighbours[s][way]
        sems = (f_send.at[s, way, k], f_recv.at[s, way, k])
        if k == 0:
            part = top if way == 0 else bottom
            return remote(g_side(s, firsts[s] + 2).at[part, :], f_first.at[s, part, :], *sems, device)
        to = firsts[s] + (1 if way == 0 else -1)
        return remote(g_side(s, to), f_buf.at[s, way], *sems, device)

    def s_copy(s, way, k):
        device = neighbours[1 - s][way]
        sems = (s_send.at[s, way, k], s_recv.at[s, way, k])
        if k == 0:
            part = sub_top if way == 0 else sub_bottom
            source = e_sum.at[s, sub_rows(seconds[s] + 2), :].at[part, :]
            return remote(source, s_first.at[s, part, :], *sems, device)
        to = seconds[s] + (1 if way == 0 else -1)
        return remote(e_sum.at[s, sub_rows(to), :], s_buf.at[s, way], *sems, device)

    def f_pass(s):
        for way in range(2):
            f_copy(s, way, 0).wait_recv()
            part = top if way == 0 else bottom
            own = g_side(s, firsts[s] + (1 if way == 0 else -1)).at[part, :]
            sum_into(own, [own, f_first.at[s, part, :]])
            f_copy(s, way, 1).start()

    def f_final(s):
        for way in range(2):
            f_copy(s, way, 1).wait_recv()
        sum_into(e_sum.at[s], [g_side(s, firsts[s]), f_buf.at[s, 0], f_buf.at[s, 1]])
        for way in range(2):
            s_copy(s, way, 0).start()

    def s_pass(s):
        for way in range(2):
            s_copy(s, way, 0).wait_recv()
            part = sub_top if way == 0 else sub_bottom
            to = seconds[s] + (1 if way == 0 else -1)
            own = e_sum.at[s, sub_rows(to), :].at[part, :]
            sum_into(own, [own, s_first.at[s, part, :]])
            s_copy(s, way, 1).start()

    def work(s, row, col, count=sub, first=0):
        start = pl.multiple_of(s * side_rows + ((row + 4) % 4) * sub + first, 16)
        return g_work.at[pl.ds(start, count), columns(col)]

    def work_column(s, col):
        return g_work.at[pl.ds(s * side_rows, side_rows), columns(col)]

    def s_final(s):
        for way in range(2):
            s_copy(s, way, 1).wait_recv()
        own = e_sum.at[s, sub_rows(seconds[s]), :]
        sum_into(work(s, seconds[s], firsts[s]), [own, s_buf.at[s, 0], s_buf.at[s, 1]])

    def ya(s, way, k):
        device = north if way == 0 else south
        if s == 0:
            if k == 0:
                spot = work(0, y, x)
            else:
                count, first = (48, 0) if way == 0 else (32, 48)
                spot = work(0, y - 1 if way == 0 else y + 1, x, count, first)
        else:
            if k == 0:
                spot = work_column(1, y)
            else:
                part = top if way == 0 else bottom
                spot = work_column(1, y - 1 if way == 0 else y + 1).at[part, :]
        return remote(spot, spot, ga_send.at[s, way, k], ga_recv.at[s, way, k], device)

    def xa(s, i):
        spot = work_column(0, x) if s == 0 else work(1, x, y)
        return remote(spot, spot, gh_send.at[s, i], gh_recv.at[s, i], (right, left, across)[i])

    def xa_came(s, i):
        source = (x - 1, x + 1, x + 2)[i]
        spot = work_column(0, source) if s == 0 else work(1, source, y)
        return remote(spot, spot, gh_send.at[s, i], gh_recv.at[s, i], pair)

    def xa_start(s):
        @pl.when(place.away)
        def _():
            xa(s, 0).start()
            xa(s, 1).start()

        @pl.when(place.home)
        def _():
            xa(s, 2).start()

    def handed(s, i):
        at = x if s == 0 else y
        return (pl.ds(s * side_rows, side_rows), columns((at, at - 1, at + 1, at + 2)[i]))

    def hand_pair(s, i):
        spot = handed(s, i)
        return remote(g_work.at[spot], g_out.at[spot], go_send.at[s, i], go_recv.at[s, i], pair)

    def hand_out(s, i):
        spot = handed(s, i)
        return pltpu.make_async_copy(g_work.at[spot], g_out.at[spot], go_local.at[s, i])

    def hand(s, i):
        hand_pair(s, i).start()
        hand_out(s, i).start()

    for s in range(2):
        for way in range(2):
            f_copy(s, way, 0).start()
    z_round(0, 3)

    def back_parts(j):
        here = pl.ds(pl.multiple_of(j * 256, 256), 256)
        for i in range(10):
            cols = slice(i * 256, (i + 1) * 256)
            backs[here, cols] = nn(dqkv[here, :], wq[:, cols]).astype(LOW)

    loop(4, back_parts)
    for j in order:
        core_copy(1, j).start()
    z_round(1, 0)
    for s in range(2):
        f_pass(s)
    z_final(0)
    z_round(1, 1)
    for s in range(2):
        f_final(s)
    z_round(1, 2)
    for s in range(2):
        s_pass(s)
    for s in (1, 0):
        s_final(s)
        if s == 0:
            for way in range(2):
                ya(0, way, 0).start()
        else:
            xa_start(1)
    for way in range(2):
        ya(0, way, 0).wait_recv()
        ya(0, way, 1).start()
    z_round(1, 3)
    for way in range(2):
        ya(0, way, 1).wait_recv()
    xa_start(0)

    @pl.when(place.home)
    def _():
        for i in range(3):
            xa_came(1, i).wait_recv()
        for way in range(2):
            ya(1, way, 0).start()
        hand(1, 0)
        hand(0, 0)
        for way in range(2):
            ya(1, way, 0).wait_recv()
            ya(1, way, 1).start()
            hand(1, 1 + way)

    def landing(a):
        @pl.when(place.away)
        def _():
            swap_back(a).wait_recv()

        @pl.when(place.home)
        def _():
            keep_back(a).wait()

    def finish_output(i):
        here = pl.ds(pl.multiple_of(i * 16, 16), 16)
        out_ref[here, :] = (tokens[here, :].astype(WIDE) + landed[0, here, :].astype(WIDE)).astype(LOW)

    def finish_gradient(i):
        here = pl.ds(pl.multiple_of(i * 16, 16), 16)
        xhat, rstd = standardize(tokens[here, :])
        scaled = landed[1, here, :].astype(WIDE) * gain[...]
        first = jnp.mean(scaled, axis=-1, keepdims=True)
        second = jnp.mean(scaled * xhat, axis=-1, keepdims=True)
        total = cot[here, :].astype(WIDE) + rstd * (scaled - first - xhat * second)
        ingrad_ref[here, :] = total.astype(LOW)

    landing(0)
    loop(rows // 16, finish_output)
    z_final(1)

    @pl.when(place.home)
    def _():
        for way in range(2):
            ya(1, way, 1).wait_recv()
        hand(1, 3)
        for i in range(3):
            xa_came(0, i).wait_recv()
            hand(0, 1 + i)

    landing(1)
    loop(rows // 16, finish_gradient)

    @pl.when(place.away)
    def _():
        for s in range(2):
            for i in range(4):
                hand_pair(s, i).wait_recv()
            xa(s, 0).wait_send()
            xa(s, 1).wait_send()
        for a in range(2):
            swap(a).wait_send()
            swap_back(a).wait_send()
        for i, h in weights:
            weight_swap(i, h).wait_send()

    @pl.when(place.home)
    def _():
        for s in range(2):
            for i in range(4):
                hand_pair(s, i).wait_send()
                hand_out(s, i).wait()
            xa(s, 2).wait_send()
        for way in range(2):
            for k in range(2):
                ya(1, way, k).wait_send()

    for a in range(2):
        for i in range(9):
            to_pair(a, i).wait_send()
        for j in order:
            core_copy(a, j).wait_send()
        for way in range(2):
            for k in range(4):
                gather(a, way, k).wait_send()
                ring(a, way, k).wait_send()
    for way in range(2):
        for k in range(2):
            ya(0, way, k).wait_send()
            for s in range(2):
                f_copy(s, way, k).wait_send()
                s_copy(s, way, k).wait_send()


def run_layer(tokens, gain, w_qkv, w_out, cotangent):
    rows, dim = tokens.shape
    vmem = pl.BlockSpec(memory_space=pltpu.VMEM)
    any_space = pl.BlockSpec(memory_space=pl.ANY)
    dma = pltpu.SemaphoreType.DMA
    sums = 4 * w_out.shape[0]
    quarter = dim // 4

    def low(*shape):
        return pltpu.VMEM(shape, LOW)

    return pl.pallas_call(
        layer_kernel,
        out_shape=(
            jax.ShapeDtypeStruct((rows, dim), LOW),
            jax.ShapeDtypeStruct((rows, dim), LOW),
            jax.ShapeDtypeStruct((sums, dim), LOW),
        ),
        in_specs=[vmem, vmem, any_space, any_space, vmem],
        out_specs=(vmem, vmem, any_space),
        scratch_shapes=[
            low(rows, dim),
            low(rows * 16, dim),
            low(rows * 16, dim),
            low(6 * PAD, dim),
            low(2 * PAD, dim),
            low(rows * 16, 6 * PAD),
            low(rows * 16, 2 * PAD),
            low(rows * 16, 2 * PAD),
            low(rows * 16, 6 * PAD),
            pltpu.VMEM((4, LEN, LEN), WIDE),
            pltpu.VMEM((LEN, PAD), WIDE),
            pltpu.VMEM((LEN, PAD), WIDE),
            low(rows * 16, dim),
            low(rows * 16, dim),
            low(2, 8, rows, dim),
            low(2, rows, dim),
            low(2, 2, 3, rows, dim),
            low(2, rows, dim),
            low(2, rows, dim),
            low(sums, dim),
            low(2, sums // 2, quarter),
            low(2, 2, sums // 2, quarter),
            low(2, sums // 2, quarter),
            low(2, sums // 8, quarter),
            low(2, 2, sums // 8, quarter),
            low(sums, dim),
            dma((2,)),
            dma((2,)),
            dma((2,)),
            dma((4, 2)),
            dma((4, 2)),
            dma((4, 2)),
            dma((2, 2, 4)),
            dma((2, 2, 4)),
            dma((2, 9)),
            dma((2, 9)),
            dma((2, 8)),
            dma((2, 8)),
            dma((2, 2, 4)),
            dma((2, 2, 4)),
            dma((2,)),
            dma((2,)),
            dma((2,)),
            dma((2, 2, 2)),
            dma((2, 2, 2)),
            dma((2, 2, 2)),
            dma((2, 2, 2)),
            dma((2, 2, 2)),
            dma((2, 2, 2)),
            dma((2, 3)),
            dma((2, 3)),
            dma((2, 4)),
            dma((2, 4)),
            dma((2, 4)),
        ],
        compiler_params=pltpu.CompilerParams(
            collective_id=0, has_side_effects=True, vmem_limit_bytes=VMEM_BYTES
        ),
        name="attention_layer",
    )(tokens, gain.reshape(1, dim), w_qkv, w_out, cotangent)


def per_device(tokens, gain, w_qkv, w_out, cotangent):
    width = w_out.shape[0]
    output, input_gradient, sums = run_layer(tokens, gain, w_qkv, w_out, cotangent)
    replicas = lax.axis_size("dp")
    grad_qkv = sums[: 3 * width].astype(jnp.float32) / replicas
    grad_out = sums[3 * width :].astype(jnp.float32) / replicas
    return (output, input_gradient, grad_qkv.reshape(w_qkv.shape), grad_out)


def solution(mesh):
    placed = (
        P(("dp", "tensor"), None),
        P(),
        P(None, "tensor", None),
        P("tensor", None),
        P(("dp", "tensor"), None),
    )
    return jax.shard_map(
        per_device,
        mesh=mesh,
        in_specs=placed,
        out_specs=(
            P(("dp", "tensor"), None),
            P(("dp", "tensor"), None),
            P(None, "tensor", None),
            P("tensor", None),
        ),
        check_vma=False,
    )
```

time: 710 us -> 163 us (0.23)
  waiting for transfers between devices: 612 us -> 0 us
  Pallas kernels: 0 us -> 153 us
  matrix products: 59.1 us -> 0 us
  between operations: 14 us -> 0.64 us
  other arithmetic: 16.1 us -> 7.14 us
    reduce_scatter x2 -> x0, waiting for transfers between devices: 237 us -> none  [the longest x1 121 us: per_device(): lax.psum_scatter(jnp.dot(att_flat, w_out, preferred_element_type=jnp.floa...]
    all_gather x2 -> x0, waiting for transfers between devices: 232 us -> none  [the longest x1 121 us: per_device(): lax.all_gather(normalized_rows, 'tensor', axis=0, tiled=True)]
    pallas_call x0 -> x1, Pallas kernels: none -> 153 us  [run_layer(): pl.pallas_call(layer_kernel, out_shape=(jax.ShapeDtypeStruct((rows, dim),...]
    psum x1 -> x0, waiting for transfers between devices: 142 us -> none  [sum_weights(): lax.psum(grad_qkv_part.astype(jnp.bfloat16), 'dp').astype(jnp.float32)]
    dot_general x11 -> x0, matrix products: 54.2 us -> none  [the longest x2 10.7 us: inner_cols(): lax.dot_general(left, right, (((1,), (1,)), ((), ())), preferred_element_...]
  transfers between devices with their start and end apart: 5 -> 0, of which waited for: 5 -> 0; matrix products, arithmetic and copies ran while one was open for 4% -> 0% of each run, Pallas kernels for 0% -> 0%
where the time goes in v2:
time: 163 us
  Pallas kernels  153 us (94%)
  other arithmetic  7.14 us (4%)
  local copies, waits for them, and re-layouts  2.77 us (2%)
    pallas_call x1, Pallas kernels, run_layer(): pl.pallas_call(layer_kernel, out_shape=(jax.ShapeDtypeStruct((rows, dim),...  153 us
    div x1, other arithmetic, per_device(): grad_qkv = sums[:3 * width].astype(jnp.float32) / replicas  4.66 us

profile of v2, /device:TPU:1, one launch (start us, length us, event | category | flops | bytes accessed | tf_op | source)
XLA Modules:
  0.0 163.3 jit_solution(15362726521920360071)
XLA Ops:
  0.6 1.3 reshape.14.gain
  1.9 152.7 %attention_layer.1 = (bf16[64,2560]{1,0:T(8,128)(2,1)}, bf16[64,2560]{1,0:T(8,128)(2,1)}, bf16[640,2560]{1,0:T(8,128)(2,1)}) custom-call(bf16[64,2560]{1,0:T(8,128)(2,1)} %tokens.1, f32[1,2560]{1,0:T(1,128)} %reshape.14.gain, bf16[3,160,2560]{2,1,0:T(8,128)(2,1)} %wq_ref.1, bf16[160,2560]{1,0:T(8,128)(2,1)} %wo_ref.1, bf16[64,2560]{1,0:T(8,128)(2,1)} %cot.1), custom_call_target="tpu_custom_call" | custom-call | tf_op jit(solution)/shard_map/attention_layer/pallas_call | solution.py:745
  154.7 2.5 %convert_multiply_fusion.1 = f32[160,2560]{1,0:T(8,128)} fusion(bf16[640,2560]{1,0:T(8,128)(2,1)} %get-tuple-element.9), kind=kLoop, calls=%fused_computation.1 | loop fusion | flops 819200 | bytes 2457600 | tf_op jit(solution)/shard_map/div | solution.py:822
  157.1 0.0 copy-start.1
  157.1 0.0 copy-start
  157.2 4.7 %convert_multiply_fusion = f32[480,2560]{1,0:T(8,128)} fusion(bf16[640,2560]{1,0:T(8,128)(2,1)} %get-tuple-element.9), kind=kLoop, calls=%fused_computation | loop fusion | flops 2457600 | bytes 7372800 | tf_op jit(solution)/shard_map/div | solution.py:821
  161.8 0.0 copy-done.1
  161.8 0.7 copy.11
  162.5 0.0 copy-done
  162.5 0.7 copy.12
Async XLA Ops:
  157.1 4.7 %copy-start.1 = (bf16[64,2560]{1,0:T(8,128)(2,1)S(1)}, bf16[64,2560]{1,0:T(8,128)(2,1)}, u32[]{:S(2)}) copy-start(bf16[64,2560]{1,0:T(8,128)(2,1)} %get-tuple-element.14) | copy-start | bytes 983044
  157.1 5.4 %copy-start = (bf16[64,2560]{1,0:T(8,128)(2,1)S(1)}, bf16[64,2560]{1,0:T(8,128)(2,1)}, u32[]{:S(2)}) copy-start(bf16[64,2560]{1,0:T(8,128)(2,1)} %get-tuple-element.15) | copy-start | bytes 983044

commit v3 on v2

v3 whole, which is shorter than its diff:
```python
import jax
import jax.numpy as jnp
from jax import lax
from jax.experimental import pallas as pl
from jax.experimental.pallas import tpu as pltpu
from jax.sharding import PartitionSpec as P

HEAD_DIM = 80
LEN = 512
PAD = 128
BLOCK = 64
SCALE = HEAD_DIM ** (-0.5)
MESH = pl.DeviceIdType.MESH
VMEM_BYTES = 60 * 1024 * 1024
LOW = jnp.bfloat16
WIDE = jnp.float32


class Place:
    def __init__(self):
        dp, tensor = lax.axis_index("dp"), lax.axis_index("tensor")
        self.core = dp % 2
        self.y = (dp // 2) % 4
        self.x_lo = tensor % 2
        self.x = (dp // 8) * 2 + self.x_lo
        self.z = tensor // 2
        self.home = self.core == self.x_lo
        self.away = self.core != self.x_lo

    def at(self, x=None, y=None, z=None, core=None):
        x = self.x if x is None else x
        y = self.y if y is None else y
        z = self.z if z is None else z
        core = self.core if core is None else core
        return ((x // 2) * 8 + y * 2 + core, z * 2 + x % 2)

    def pair(self):
        return self.at(core=1 - self.core)

    def crossed(self, by):
        return self.at(x=(self.x + by + 4) % 4, core=1 - self.core)

    def partner(self):
        return self.crossed(1 - 2 * self.x_lo)

    def z_next(self, by):
        return self.at(z=(self.z + by + 8) % 8)

    def x_next(self, by):
        return self.at(x=(self.x + by + 4) % 4)

    def y_next(self, by):
        return self.at(y=(self.y + by + 4) % 4)


def greet(devices):
    barrier = pltpu.get_barrier_semaphore()
    for device in devices:
        pl.semaphore_signal(barrier, inc=1, device_id=device, device_id_type=MESH)
    pl.semaphore_wait(barrier, len(devices))


def remote(source, target, send_sem, recv_sem, device):
    return pltpu.make_async_remote_copy(
        src_ref=source,
        dst_ref=target,
        send_sem=send_sem,
        recv_sem=recv_sem,
        device_id=device,
        device_id_type=MESH,
    )


def sum_into(target, terms):
    def step(i, carry):
        here = pl.ds(pl.multiple_of(i * 16, 16), 16)
        total = terms[0][here, :].astype(jnp.float32)
        for term in terms[1:]:
            total = total + term[here, :].astype(jnp.float32)
        target[here, :] = total.astype(jnp.bfloat16)
        return carry

    lax.fori_loop(0, target.shape[0] // 16, step, 0)


def nt(left, right):
    return lax.dot_general(left, right, (((1,), (1,)), ((), ())), preferred_element_type=WIDE)


def tn(left, right):
    return lax.dot_general(left, right, (((0,), (0,)), ((), ())), preferred_element_type=WIDE)


def nn(left, right):
    return jnp.dot(left, right, preferred_element_type=WIDE)


def standardize(x):
    xf = x.astype(WIDE)
    centered = xf - jnp.mean(xf, axis=-1, keepdims=True)
    var = jnp.mean(centered * centered, axis=-1, keepdims=True)
    rstd = lax.rsqrt(var + 1e-05)
    return centered * rstd, rstd


def loop(count, body):
    def step(i, carry):
        body(i)
        return carry

    lax.fori_loop(0, count, step, 0)


def layer_kernel(
    tokens,
    gain,
    wq_ref,
    wo_ref,
    cot,
    out_ref,
    ingrad_ref,
    g_out,
    stage,
    x_full,
    c_full,
    wq,
    wo,
    qkv,
    att,
    datt,
    dqkv,
    probs,
    dk_sum,
    dv_sum,
    parts,
    backs,
    theirs,
    first_buf,
    ring_buf,
    final,
    landed,
    g,
    f_first,
    f_buf,
    e_sum,
    s_first,
    s_buf,
    g_work,
    local_sem,
    swap_send,
    swap_recv,
    w_local,
    w_send,
    w_recv,
    gr_send,
    gr_recv,
    go_pair_send,
    go_pair_recv,
    gp_send,
    gp_recv,
    core_send,
    core_recv,
    ring_send,
    ring_recv,
    back_send,
    back_recv,
    back_local,
    f_send,
    f_recv,
    s_send,
    s_recv,
    ga_send,
    ga_recv,
    gh_send,
    gh_recv,
    go_send,
    go_recv,
    go_local,
):
    place = Place()
    x, y, z, core = place.x, place.y, place.z, place.core
    dim = tokens.shape[1]
    rows = BLOCK
    half = rows // 2
    up, down = place.z_next(1), place.z_next(-1)
    pair, partner = place.pair(), place.partner()
    right, left, across = place.x_next(1), place.x_next(-1), place.x_next(2)
    north, south = place.y_next(1), place.y_next(-1)
    cross_right, cross_left = place.crossed(1), place.crossed(-1)

    for i in range(6):
        wq[i * PAD + HEAD_DIM : (i + 1) * PAD, :] = jnp.zeros((PAD - HEAD_DIM, dim), LOW)
    for i in range(2):
        wo[i * PAD + HEAD_DIM : (i + 1) * PAD, :] = jnp.zeros((PAD - HEAD_DIM, dim), LOW)

    def norm_rows(i):
        here = pl.ds(pl.multiple_of(i * 16, 16), 16)
        xhat, _ = standardize(tokens[here, :])
        stage[here, :] = (xhat * gain[...]).astype(LOW)

    loop(rows // 16, norm_rows)
    greet([up, down, pair, cross_right, cross_left, right, left, across, north, south])

    def block(full, owner, side, first=0, count=rows):
        owner = (owner + 8) % 8
        start = pl.multiple_of((owner * 2 + side) * rows + first, 32)
        return full.at[pl.ds(start, count), :]

    chunks = (slice(0, half), slice(half, rows))
    both = ((0, 0), (0, 1), (1, 0), (1, 1))
    fulls, owned = (x_full, c_full), (stage, cot)

    def hops(way, q):
        return 4 if way == q else 3

    def swap(a, q):
        target = block(fulls[a], z, 1 - core, q * half, half)
        source = owned[a].at[chunks[q], :]
        return remote(source, target, swap_send.at[a, q], swap_recv.at[a, q], partner)

    def keep(a, q):
        target = block(fulls[a], z, core, q * half, half)
        return pltpu.make_async_copy(owned[a].at[chunks[q], :], target, local_sem.at[a, q])

    def weight_ends(i, h):
        if i < 3:
            source = wq_ref.at[i, pl.ds(h * HEAD_DIM, HEAD_DIM), :]
            return source, wq.at[pl.ds((2 * i + h) * PAD, HEAD_DIM), :]
        return wo_ref.at[pl.ds(h * HEAD_DIM, HEAD_DIM), :], wo.at[pl.ds(h * PAD, HEAD_DIM), :]

    def weight_swap(i, h):
        device = cross_right if h == 0 else cross_left
        return remote(*weight_ends(i, h), w_send.at[i, h], w_recv.at[i, h], device)

    def weight_keep(i, h):
        return pltpu.make_async_copy(*weight_ends(i, h), w_local.at[i, h])

    weights = [(i, h) for i in range(4) for h in range(2)]

    @pl.when(place.away)
    def _():
        for a, q in both:
            swap(a, q).start()
        for i, h in weights:
            weight_swap(i, h).start()

    @pl.when(place.home)
    def _():
        for a, q in both:
            keep(a, q).start()
        for i, h in weights:
            weight_keep(i, h).start()

    def gather_piece(a, way, hop, q):
        return block(fulls[a], z - hop if way == 0 else z + hop, core, q * half, half)

    def gather(a, way, k, q):
        piece = gather_piece(a, way, k, q)
        device = up if way == 0 else down
        return remote(piece, piece, gr_send.at[a, way, k, q], gr_recv.at[a, way, k, q], device)

    def own_pair(a, q):
        piece = gather_piece(a, 0, 0, q)
        return remote(piece, piece, go_pair_send.at[a, q], go_pair_recv.at[a, q], pair)

    def to_pair(a, way, k, q):
        piece = gather_piece(a, way, k + 1, q)
        return remote(piece, piece, gp_send.at[a, way, k, q], gp_recv.at[a, way, k, q], pair)

    def begin(a, q):
        @pl.when(place.away)
        def _():
            swap(a, q).wait_recv()

        @pl.when(place.home)
        def _():
            keep(a, q).wait()

        for way in range(2):
            gather(a, way, 0, q).start()
        own_pair(a, q).start()

    def advance(a, k, q):
        for way in range(2):
            if k < hops(way, q):
                gather(a, way, k, q).wait_recv()
                if k + 1 < hops(way, q):
                    gather(a, way, k + 1, q).start()
                to_pair(a, way, k, q).start()

    hop_list = [(way, k, q) for k in range(4) for q in range(2) for way in range(2) if k < hops(way, q)]

    def gathered(a):
        for q in range(2):
            own_pair(a, q).wait_recv()
        for way, k, q in hop_list:
            to_pair(a, way, k, q).wait_recv()

    for q in range(2):
        begin(0, q)
    for k in range(3):
        for q in range(2):
            advance(0, k, q)
    for q in range(2):
        begin(1, q)
    for q in range(2):
        advance(0, 3, q)

    @pl.when(place.away)
    def _():
        for i, h in weights:
            weight_swap(i, h).wait_recv()

    @pl.when(place.home)
    def _():
        for i, h in weights:
            weight_keep(i, h).wait()

    gathered(0)

    def project(j):
        here = pl.ds(pl.multiple_of(j * 256, 256), 256)
        for i in range(3):
            cols = slice(i * 256, (i + 1) * 256)
            qkv[here, cols] = nt(x_full[here, :], wq[cols, :]).astype(LOW)

    def spots(u):
        r0 = pl.multiple_of((u // 2) * LEN, LEN)
        c0 = pl.multiple_of((u % 2) * PAD, PAD)
        return r0, c0

    def forward(u):
        r0, c0 = spots(u)
        for i in range(4):
            n = (i + 1) * 128
            here = pl.ds(r0 + i * 128, 128)
            query = qkv[here, pl.ds(c0, PAD)]
            key = qkv[pl.ds(r0, n), pl.ds(c0 + 256, PAD)]
            value = qkv[pl.ds(r0, n), pl.ds(c0 + 512, PAD)]
            scores = nt(query, key) * SCALE
            q_at = lax.broadcasted_iota(jnp.int32, (128, n), 0) + i * 128
            k_at = lax.broadcasted_iota(jnp.int32, (128, n), 1)
            scores = jnp.where(q_at >= k_at, scores, -1e30)
            expo = jnp.exp(scores - jnp.max(scores, axis=-1, keepdims=True))
            p = expo * (1.0 / jnp.sum(expo, axis=-1, keepdims=True))
            probs[u, i * 128 : (i + 1) * 128, :n] = p
            att[here, pl.ds(c0, PAD)] = nn(p.astype(LOW), value).astype(LOW)

    def one(at, body):
        loop(1, lambda i: body(at + i))

    def two(first, body):
        loop(2, lambda i: body(first + i))

    def out_parts(j):
        here = pl.ds(pl.multiple_of(j * 256, 256), 256)
        for i in range(10):
            cols = slice(i * 256, (i + 1) * 256)
            parts[here, cols] = nn(att[here, :], wo[:, cols]).astype(LOW)

    sources = (parts, backs)
    near = ((z + 4) % 8) // 2
    groups = (near, (near + 1) % 4, (near + 3) % 4, (near + 2) % 4)
    order = (4, 3, -3, 2, -2, 1, -1, 0)

    def core_copy(a, j):
        owner = (z + j + 8) % 8
        source = block(sources[a], owner, 1 - core)
        return remote(
            source, theirs.at[a, owner], core_send.at[a, j + 3], core_recv.at[a, j + 3], pair
        )

    def ring(a, way, k, q):
        sign = 1 if way == 0 else -1
        owner = (z + sign * (4 - k) + 8) % 8
        source = theirs.at[a, owner, chunks[q], :]
        if k == 0:
            target = first_buf.at[a, chunks[q], :]
        else:
            target = ring_buf.at[a, way, k - 1, chunks[q], :]
        device = up if way == 0 else down
        return remote(source, target, ring_send.at[a, way, k, q], ring_recv.at[a, way, k, q], device)

    def z_step(a, k, q):
        for way in range(2):
            if k < 4 - hops(way, q):
                continue
            j = (4 - k) * (1 if way == 0 else -1)
            owner = (z + j + 8) % 8
            own = block(sources[a], owner, core, q * half, half)
            other = theirs.at[a, owner, chunks[q], :]
            terms = [own, other]
            if k == 0:
                if q == 0:
                    core_copy(a, 4).wait_recv()
            else:
                if q == 0:
                    core_copy(a, j).wait_recv()
                if k > 4 - hops(way, q):
                    ring(a, way, k - 1, q).wait_recv()
                    if k == 1:
                        terms.append(first_buf.at[a, chunks[q], :])
                    else:
                        terms.append(ring_buf.at[a, way, k - 2, chunks[q], :])
            sum_into(other, terms)
            ring(a, way, k, q).start()

    send_list = [(way, k, q) for k in range(4) for q in range(2) for way in range(2) if k >= 4 - hops(way, q)]

    def swap_back(a, q):
        source, target = final.at[a, chunks[q], :], landed.at[a, chunks[q], :]
        return remote(source, target, back_send.at[a, q], back_recv.at[a, q], partner)

    def keep_back(a, q):
        source, target = final.at[a, chunks[q], :], landed.at[a, chunks[q], :]
        return pltpu.make_async_copy(source, target, back_local.at[a, q])

    def z_final(a, q):
        if q == 0:
            core_copy(a, 0).wait_recv()
        terms = [block(sources[a], z, core, q * half, half), theirs.at[a, z, chunks[q], :]]
        for way in range(2):
            ring(a, way, 3, q).wait_recv()
            terms.append(ring_buf.at[a, way, 2, chunks[q], :])
        sum_into(final.at[a, chunks[q], :], terms)

        @pl.when(place.away)
        def _():
            swap_back(a, q).start()

        @pl.when(place.home)
        def _():
            keep_back(a, q).start()

    def core_copies(a, js):
        for j in js:
            core_copy(a, j).start()

    one(0, project)
    advance(1, 0, 0)
    one(1, project)
    advance(1, 0, 1)
    one(2, project)
    advance(1, 1, 0)
    one(3, project)
    advance(1, 1, 1)
    one(0, forward)
    one(1, forward)
    advance(1, 2, 0)
    one(2, forward)
    one(3, forward)
    advance(1, 2, 1)
    one(groups[0], out_parts)
    core_copies(0, (4,))
    one(groups[1], out_parts)
    one(groups[2], out_parts)
    core_copies(0, (3, -3, 2, -2))
    z_step(0, 0, 0)
    z_step(0, 0, 1)
    one(groups[3], out_parts)
    core_copies(0, (1, -1, 0))
    advance(1, 3, 0)
    advance(1, 3, 1)
    gathered(1)

    def project_back(j):
        here = pl.ds(pl.multiple_of(j * 256, 256), 256)
        datt[here, :] = nt(c_full[here, :], wo[...]).astype(LOW)

    def backward(u):
        r0, c0 = spots(u)
        for i in (3, 2, 1, 0):
            n = (i + 1) * 128
            here = pl.ds(r0 + i * 128, 128)
            query = qkv[here, pl.ds(c0, PAD)]
            key = qkv[pl.ds(r0, n), pl.ds(c0 + 256, PAD)]
            value = qkv[pl.ds(r0, n), pl.ds(c0 + 512, PAD)]
            d_att = datt[here, pl.ds(c0, PAD)]
            p = probs[u, i * 128 : (i + 1) * 128, :n]
            d_probs = nt(d_att, value)
            d_score = p * (d_probs - jnp.sum(d_probs * p, axis=-1, keepdims=True)) * SCALE
            d_low = d_score.astype(LOW)
            dqkv[here, pl.ds(c0, PAD)] = nn(d_low, key).astype(LOW)
            dk, dv = tn(d_low, query), tn(p.astype(LOW), d_att)
            if i == 3:
                dk_sum[...] = dk
                dv_sum[...] = dv
            else:
                dk_sum[:n, :] += dk
                dv_sum[:n, :] += dv
        dqkv[pl.ds(r0, LEN), pl.ds(c0 + 256, PAD)] = dk_sum[...].astype(LOW)
        dqkv[pl.ds(r0, LEN), pl.ds(c0 + 512, PAD)] = dv_sum[...].astype(LOW)

    loop(4, project_back)
    z_step(0, 1, 0)
    one(0, backward)
    z_step(0, 1, 1)
    two(1, backward)
    z_step(0, 2, 0)
    one(3, backward)
    z_step(0, 2, 1)

    for j in range(4):
        lanes = slice(j * 256, (j + 1) * 256)
        for i in range(3):
            backs[i * 256 : (i + 1) * 256, lanes] = dqkv[lanes, i * 256 : (i + 1) * 256].T
        backs[768:1024, lanes] = att[lanes, :].T

    def weight_grads(j):
        cols = pl.ds(pl.multiple_of(j * 256, 256), 256)
        for i in range(4):
            factor = backs[i * 256 : (i + 1) * 256, 0:1024]
            total = nn(factor, (x_full if i < 3 else c_full)[:, cols]).astype(LOW)
            for h in range(2):
                spot = i * 160 + h * HEAD_DIM
                g[spot : spot + HEAD_DIM, cols] = total[h * PAD : h * PAD + HEAD_DIM, :]

    two(0, weight_grads)
    z_step(0, 3, 0)
    loop(8, lambda j: weight_grads(j + 2))

    side_start, side_rows, subs, width = (0, 256), (256, 384), (64, 96), dim // 4
    firsts, seconds = (x, y), (y, x)
    neighbours = ((right, left), (north, south))
    lanes = (slice(0, 384), slice(384, 640))
    pieces = [(s, c) for c in range(2) for s in range(2)]

    def half_of(s, way, size):
        count = size[s] // 2
        return slice(way * count, (way + 1) * count)

    def columns(q):
        return pl.ds(pl.multiple_of(((q + 4) % 4) * width, 128), width)

    def g_side(s, q, c):
        return g.at[pl.ds(side_start[s], side_rows[s]), columns(q)].at[:, lanes[c]]

    def sub_rows(s, q):
        return pl.ds(pl.multiple_of(((q + 4) % 4) * subs[s], 32), subs[s])

    def e_sub(s, q, c):
        return e_sum.at[s, sub_rows(s, q), lanes[c]]

    def step_to(s, way, places):
        return places[s] + (1 if way == 0 else -1)

    def f_copy(s, way, k, c):
        device = neighbours[s][way]
        sems = (f_send.at[s, way, k, c], f_recv.at[s, way, k, c])
        if k == 0:
            part = half_of(s, way, side_rows)
            source = g_side(s, firsts[s] + 2, c).at[part, :]
            return remote(source, f_first.at[s, part, lanes[c]], *sems, device)
        source = g_side(s, step_to(s, way, firsts), c)
        return remote(source, f_buf.at[s, way, 0 : side_rows[s], lanes[c]], *sems, device)

    def s_copy(s, way, k, c):
        device = neighbours[1 - s][way]
        sems = (s_send.at[s, way, k, c], s_recv.at[s, way, k, c])
        if k == 0:
            part = half_of(s, way, subs)
            source = e_sub(s, seconds[s] + 2, c).at[part, :]
            return remote(source, s_first.at[s, part, lanes[c]], *sems, device)
        source = e_sub(s, step_to(s, way, seconds), c)
        return remote(source, s_buf.at[s, way, 0 : subs[s], lanes[c]], *sems, device)

    def f_pass(s, c):
        for way in range(2):
            f_copy(s, way, 0, c).wait_recv()
            part = half_of(s, way, side_rows)
            own = g_side(s, step_to(s, way, firsts), c).at[part, :]
            sum_into(own, [own, f_first.at[s, part, lanes[c]]])
            f_copy(s, way, 1, c).start()

    def f_final(s, c):
        for way in range(2):
            f_copy(s, way, 1, c).wait_recv()
        came = [f_buf.at[s, way, 0 : side_rows[s], lanes[c]] for way in range(2)]
        sum_into(e_sum.at[s, 0 : side_rows[s], lanes[c]], [g_side(s, firsts[s], c)] + came)
        for way in range(2):
            s_copy(s, way, 0, c).start()

    def s_pass(s, c):
        for way in range(2):
            s_copy(s, way, 0, c).wait_recv()
            part = half_of(s, way, subs)
            own = e_sub(s, step_to(s, way, seconds), c).at[part, :]
            sum_into(own, [own, s_first.at[s, part, lanes[c]]])
            s_copy(s, way, 1, c).start()

    def work(s, row, col, c):
        start = pl.multiple_of(side_start[s] + ((row + 4) % 4) * subs[s], 32)
        return g_work.at[pl.ds(start, subs[s]), columns(col)].at[:, lanes[c]]

    def work_column(s, col, c):
        return g_work.at[pl.ds(side_start[s], side_rows[s]), columns(col)].at[:, lanes[c]]

    def s_final(s, c):
        for way in range(2):
            s_copy(s, way, 1, c).wait_recv()
        came = [s_buf.at[s, way, 0 : subs[s], lanes[c]] for way in range(2)]
        sum_into(work(s, seconds[s], firsts[s], c), [e_sub(s, seconds[s], c)] + came)

    def ya(s, way, k, c):
        device = north if way == 0 else south
        at = y if k == 0 else (y - 1 if way == 0 else y + 1)
        if s == 0:
            spot, size = work(0, at, x, c), subs
        else:
            spot, size = work_column(1, at, c), side_rows
        if k == 1:
            spot = spot.at[half_of(s, way, size), :]
        return remote(spot, spot, ga_send.at[s, way, k, c], ga_recv.at[s, way, k, c], device)

    def xa(s, i, c):
        spot = work_column(0, x, c) if s == 0 else work(1, x, y, c)
        device = (right, left, across)[i]
        return remote(spot, spot, gh_send.at[s, i, c], gh_recv.at[s, i, c], device)

    def xa_came(s, i, c):
        source = (x - 1, x + 1, x + 2)[i]
        spot = work_column(0, source, c) if s == 0 else work(1, source, y, c)
        return remote(spot, spot, gh_send.at[s, i, c], gh_recv.at[s, i, c], pair)

    def xa_start(s, c):
        @pl.when(place.away)
        def _():
            xa(s, 0, c).start()
            xa(s, 1, c).start()

        @pl.when(place.home)
        def _():
            xa(s, 2, c).start()

    def handed(s, i, c):
        at = x if s == 0 else y
        place_of = columns((at, at - 1, at + 1, at + 2)[i])
        return lambda ref: ref.at[pl.ds(side_start[s], side_rows[s]), place_of].at[:, lanes[c]]

    def hand_pair(s, i, c):
        spot = handed(s, i, c)
        return remote(spot(g_work), spot(g_out), go_send.at[s, i, c], go_recv.at[s, i, c], pair)

    def hand_out(s, i, c):
        spot = handed(s, i, c)
        return pltpu.make_async_copy(spot(g_work), spot(g_out), go_local.at[s, i, c])

    def hand(s, i, c):
        hand_pair(s, i, c).start()
        hand_out(s, i, c).start()

    def y_start(c):
        for way in range(2):
            ya(0, way, 0, c).start()
        xa_start(1, c)

    def y_pass(c):
        for way in range(2):
            ya(0, way, 0, c).wait_recv()
            ya(0, way, 1, c).start()

    def y_final(c):
        for way in range(2):
            ya(0, way, 1, c).wait_recv()
        xa_start(0, c)

    for s, c in pieces:
        for way in range(2):
            f_copy(s, way, 0, c).start()

    def back_parts(j):
        here = pl.ds(pl.multiple_of(j * 256, 256), 256)
        for i in range(10):
            cols = slice(i * 256, (i + 1) * 256)
            backs[here, cols] = nn(dqkv[here, :], wq[:, cols]).astype(LOW)

    z_step(0, 3, 1)
    one(groups[0], back_parts)
    core_copies(1, (4,))
    f_pass(0, 0)
    f_pass(1, 0)
    one(groups[1], back_parts)
    z_step(1, 0, 0)
    z_step(1, 0, 1)
    one(groups[2], back_parts)
    core_copies(1, (3, -3, 2, -2))
    f_pass(0, 1)
    f_pass(1, 1)
    z_final(0, 0)
    z_step(1, 1, 0)
    one(groups[3], back_parts)
    core_copies(1, (1, -1, 0))
    z_final(0, 1)
    z_step(1, 1, 1)
    f_final(0, 0)
    f_final(1, 0)
    z_step(1, 2, 0)
    s_pass(0, 0)
    s_pass(1, 0)
    f_final(0, 1)
    f_final(1, 1)
    z_step(1, 2, 1)
    s_pass(0, 1)
    s_pass(1, 1)
    s_final(0, 0)
    s_final(1, 0)
    y_start(0)
    z_step(1, 3, 0)
    s_final(0, 1)
    s_final(1, 1)
    y_start(1)
    y_pass(0)
    z_step(1, 3, 1)
    y_pass(1)
    y_final(0)

    @pl.when(place.home)
    def _():
        for c in range(2):
            for i in range(3):
                xa_came(1, i, c).wait_recv()
            for way in range(2):
                ya(1, way, 0, c).start()
            hand(1, 0, c)
            if c == 0:
                hand(0, 0, 0)

    y_final(1)

    @pl.when(place.home)
    def _():
        hand(0, 0, 1)
        for c in range(2):
            for way in range(2):
                ya(1, way, 0, c).wait_recv()
                ya(1, way, 1, c).start()
                hand(1, 1 + way, c)

    def landing(a):
        @pl.when(place.away)
        def _():
            for q in range(2):
                swap_back(a, q).wait_recv()

        @pl.when(place.home)
        def _():
            for q in range(2):
                keep_back(a, q).wait()

    def finish_output(i):
        here = pl.ds(pl.multiple_of(i * 16, 16), 16)
        out_ref[here, :] = (tokens[here, :].astype(WIDE) + landed[0, here, :].astype(WIDE)).astype(LOW)

    def finish_gradient(i):
        here = pl.ds(pl.multiple_of(i * 16, 16), 16)
        xhat, rstd = standardize(tokens[here, :])
        scaled = landed[1, here, :].astype(WIDE) * gain[...]
        first = jnp.mean(scaled, axis=-1, keepdims=True)
        second = jnp.mean(scaled * xhat, axis=-1, keepdims=True)
        total = cot[here, :].astype(WIDE) + rstd * (scaled - first - xhat * second)
        ingrad_ref[here, :] = total.astype(LOW)

    landing(0)
    loop(rows // 16, finish_output)
    z_final(1, 0)
    z_final(1, 1)
    landing(1)
    loop(rows // 16, finish_gradient)

    @pl.when(place.home)
    def _():
        for c in range(2):
            for way in range(2):
                ya(1, way, 1, c).wait_recv()
            hand(1, 3, c)
        for c in range(2):
            for i in range(3):
                xa_came(0, i, c).wait_recv()
                hand(0, 1 + i, c)

    @pl.when(place.away)
    def _():
        for s, c in pieces:
            for i in range(4):
                hand_pair(s, i, c).wait_recv()
            xa(s, 0, c).wait_send()
            xa(s, 1, c).wait_send()
        for a, q in both:
            swap(a, q).wait_send()
            swap_back(a, q).wait_send()
        for i, h in weights:
            weight_swap(i, h).wait_send()

    @pl.when(place.home)
    def _():
        for s, c in pieces:
            for i in range(4):
                hand_pair(s, i, c).wait_send()
                hand_out(s, i, c).wait()
            xa(s, 2, c).wait_send()
        for way, k in both:
            for c in range(2):
                ya(1, way, k, c).wait_send()

    for a in range(2):
        for q in range(2):
            own_pair(a, q).wait_send()
        for way, k, q in hop_list:
            gather(a, way, k, q).wait_send()
            to_pair(a, way, k, q).wait_send()
        for j in order:
            core_copy(a, j).wait_send()
        for way, k, q in send_list:
            ring(a, way, k, q).wait_send()
    for way, k in both:
        for c in range(2):
            ya(0, way, k, c).wait_send()
            for s in range(2):
                f_copy(s, way, k, c).wait_send()
                s_copy(s, way, k, c).wait_send()


def run_layer(tokens, gain, w_qkv, w_out, cotangent):
    rows, dim = tokens.shape
    vmem = pl.BlockSpec(memory_space=pltpu.VMEM)
    any_space = pl.BlockSpec(memory_space=pl.ANY)
    dma = pltpu.SemaphoreType.DMA
    sums = 4 * w_out.shape[0]
    quarter = dim // 4

    def low(*shape):
        return pltpu.VMEM(shape, LOW)

    return pl.pallas_call(
        layer_kernel,
        out_shape=(
            jax.ShapeDtypeStruct((rows, dim), LOW),
            jax.ShapeDtypeStruct((rows, dim), LOW),
            jax.ShapeDtypeStruct((sums, dim), LOW),
        ),
        in_specs=[vmem, vmem, any_space, any_space, vmem],
        out_specs=(vmem, vmem, any_space),
        scratch_shapes=[
            low(rows, dim),
            low(rows * 16, dim),
            low(rows * 16, dim),
            low(6 * PAD, dim),
            low(2 * PAD, dim),
            low(rows * 16, 6 * PAD),
            low(rows * 16, 2 * PAD),
            low(rows * 16, 2 * PAD),
            low(rows * 16, 6 * PAD),
            pltpu.VMEM((4, LEN, LEN), WIDE),
            pltpu.VMEM((LEN, PAD), WIDE),
            pltpu.VMEM((LEN, PAD), WIDE),
            low(rows * 16, dim),
            low(rows * 16, dim),
            low(2, 8, rows, dim),
            low(2, rows, dim),
            low(2, 2, 3, rows, dim),
            low(2, rows, dim),
            low(2, rows, dim),
            low(sums, dim),
            low(2, 384, quarter),
            low(2, 2, 384, quarter),
            low(2, 384, quarter),
            low(2, 96, quarter),
            low(2, 2, 96, quarter),
            low(sums, dim),
            dma((2, 2)),
            dma((2, 2)),
            dma((2, 2)),
            dma((4, 2)),
            dma((4, 2)),
            dma((4, 2)),
            dma((2, 2, 4, 2)),
            dma((2, 2, 4, 2)),
            dma((2, 2)),
            dma((2, 2)),
            dma((2, 2, 4, 2)),
            dma((2, 2, 4, 2)),
            dma((2, 8)),
            dma((2, 8)),
            dma((2, 2, 4, 2)),
            dma((2, 2, 4, 2)),
            dma((2, 2)),
            dma((2, 2)),
            dma((2, 2)),
            dma((2, 2, 2, 2)),
            dma((2, 2, 2, 2)),
            dma((2, 2, 2, 2)),
            dma((2, 2, 2, 2)),
            dma((2, 2, 2, 2)),
            dma((2, 2, 2, 2)),
            dma((2, 3, 2)),
            dma((2, 3, 2)),
            dma((2, 4, 2)),
            dma((2, 4, 2)),
            dma((2, 4, 2)),
        ],
        compiler_params=pltpu.CompilerParams(
            collective_id=0, has_side_effects=True, vmem_limit_bytes=VMEM_BYTES
        ),
        name="attention_layer",
    )(tokens, gain.reshape(1, dim), w_qkv, w_out, cotangent)


def per_device(tokens, gain, w_qkv, w_out, cotangent):
    width = w_out.shape[0]
    output, input_gradient, sums = run_layer(tokens, gain, w_qkv, w_out, cotangent)
    replicas = lax.axis_size("dp")
    grad_qkv = sums[: 3 * width].astype(jnp.float32) / replicas
    grad_out = sums[3 * width :].astype(jnp.float32) / replicas
    return (output, input_gradient, grad_qkv.reshape(w_qkv.shape), grad_out)


def solution(mesh):
    placed = (
        P(("dp", "tensor"), None),
        P(),
        P(None, "tensor", None),
        P("tensor", None),
        P(("dp", "tensor"), None),
    )
    return jax.shard_map(
        per_device,
        mesh=mesh,
        in_specs=placed,
        out_specs=(
            P(("dp", "tensor"), None),
            P(("dp", "tensor"), None),
            P(None, "tensor", None),
            P("tensor", None),
        ),
        check_vma=False,
    )
```

time: 163 us -> 153 us (0.939)
  Pallas kernels: 153 us -> 142 us
    pallas_call x1, Pallas kernels: 153 us -> 142 us  [run_layer(): pl.pallas_call(layer_kernel, out_shape=(jax.ShapeDtypeStruct((rows, dim),...]
where the time goes in v3:
time: 153 us; the launch traced here: 152 us
  Pallas kernels  142 us (93%)
  other arithmetic  7.14 us (5%)
  local copies, waits for them, and re-layouts  2.77 us (2%)
    pallas_call x1, Pallas kernels, run_layer(): pl.pallas_call(layer_kernel, out_shape=(jax.ShapeDtypeStruct((rows, dim),...  142 us
    div x1, other arithmetic, per_device(): grad_qkv = sums[:3 * width].astype(jnp.float32) / replicas  4.66 us

profile of v3, /device:TPU:1, one launch (start us, length us, event | category | flops | bytes accessed | tf_op | source)
XLA Modules:
  0.0 152.4 jit_solution(730088637612576428)
XLA Ops:
  0.6 1.3 reshape.14.gain
  1.9 141.8 %attention_layer.1 = (bf16[64,2560]{1,0:T(8,128)(2,1)}, bf16[64,2560]{1,0:T(8,128)(2,1)}, bf16[640,2560]{1,0:T(8,128)(2,1)}) custom-call(bf16[64,2560]{1,0:T(8,128)(2,1)} %tokens.1, f32[1,2560]{1,0:T(1,128)} %reshape.14.gain, bf16[3,160,2560]{2,1,0:T(8,128)(2,1)} %wq_ref.1, bf16[160,2560]{1,0:T(8,128)(2,1)} %wo_ref.1, bf16[64,2560]{1,0:T(8,128)(2,1)} %cot.1), custom_call_target="tpu_custom_call" | custom-call | tf_op jit(solution)/shard_map/attention_layer/pallas_call | solution.py:834
  143.8 2.5 %convert_multiply_fusion.1 = f32[160,2560]{1,0:T(8,128)} fusion(bf16[640,2560]{1,0:T(8,128)(2,1)} %get-tuple-element.9), kind=kLoop, calls=%fused_computation.1 | loop fusion | flops 819200 | bytes 2457600 | tf_op jit(solution)/shard_map/div | solution.py:913
  146.3 0.0 copy-start.1
  146.3 0.0 copy-start
  146.3 4.7 %convert_multiply_fusion = f32[480,2560]{1,0:T(8,128)} fusion(bf16[640,2560]{1,0:T(8,128)(2,1)} %get-tuple-element.9), kind=kLoop, calls=%fused_computation | loop fusion | flops 2457600 | bytes 7372800 | tf_op jit(solution)/shard_map/div | solution.py:912
  150.9 0.0 copy-done.1
  150.9 0.7 copy.11
  151.7 0.0 copy-done
  151.7 0.7 copy.12
Async XLA Ops:
  146.3 4.7 %copy-start.1 = (bf16[64,2560]{1,0:T(8,128)(2,1)S(1)}, bf16[64,2560]{1,0:T(8,128)(2,1)}, u32[]{:S(2)}) copy-start(bf16[64,2560]{1,0:T(8,128)(2,1)} %get-tuple-element.14) | copy-start | bytes 983044
  146.3 5.4 %copy-start = (bf16[64,2560]{1,0:T(8,128)(2,1)S(1)}, bf16[64,2560]{1,0:T(8,128)(2,1)}, u32[]{:S(2)}) copy-start(bf16[64,2560]{1,0:T(8,128)(2,1)} %get-tuple-element.15) | copy-start | bytes 983044

commit v4 on v3

--- a/solution.py
+++ b/solution.py
@@ -37,11 +37,12 @@
     def pair(self):
         return self.at(core=1 - self.core)
 
-    def crossed(self, by):
-        return self.at(x=(self.x + by + 4) % 4, core=1 - self.core)
-
-    def partner(self):
-        return self.crossed(1 - 2 * self.x_lo)
+    def crossed(self, by, z_by=0):
+        x, z = (self.x + by + 4) % 4, (self.z + z_by + 8) % 8
+        return self.at(x=x, z=z, core=1 - self.core)
+
+    def partner(self, z_by=0):
+        return self.crossed(1 - 2 * self.x_lo, z_by)
 
     def z_next(self, by):
         return self.at(z=(self.z + by + 8) % 8)
@@ -57,7 +58,10 @@
     barrier = pltpu.get_barrier_semaphore()
     for device in devices:
         pl.semaphore_signal(barrier, inc=1, device_id=device, device_id_type=MESH)
-    pl.semaphore_wait(barrier, len(devices))
+
+
+def met(count):
+    pl.semaphore_wait(pltpu.get_barrier_semaphore(), count)
 
 
 def remote(source, target, send_sem, recv_sem, device):
@@ -176,6 +180,8 @@
     go_send,
     go_recv,
     go_local,
+    relay_send,
+    relay_recv,
 ):
     place = Place()
     x, y, z, core = place.x, place.y, place.z, place.core
@@ -184,9 +190,14 @@
     half = rows // 2
     up, down = place.z_next(1), place.z_next(-1)
     pair, partner = place.pair(), place.partner()
+    slant_up, slant_down = place.partner(1), place.partner(-1)
     right, left, across = place.x_next(1), place.x_next(-1), place.x_next(2)
     north, south = place.y_next(1), place.y_next(-1)
     cross_right, cross_left = place.crossed(1), place.crossed(-1)
+
+    others = [up, down, pair, cross_right, cross_left, right, left, across, north, south]
+    others += [slant_up, slant_down]
+    greet(others)
 
     for i in range(6):
         wq[i * PAD + HEAD_DIM : (i + 1) * PAD, :] = jnp.zeros((PAD - HEAD_DIM, dim), LOW)
@@ -196,10 +207,10 @@
     def norm_rows(i):
         here = pl.ds(pl.multiple_of(i * 16, 16), 16)
         xhat, _ = standardize(tokens[here, :])
-        stage[here, :] = (xhat * gain[...]).astype(LOW)
+        stage[here, :] = (xhat * gain[...].reshape(1, dim)).astype(LOW)
 
     loop(rows // 16, norm_rows)
-    greet([up, down, pair, cross_right, cross_left, right, left, across, north, south])
+    met(len(others))
 
     def block(full, owner, side, first=0, count=rows):
         owner = (owner + 8) % 8
@@ -237,15 +248,33 @@
 
     weights = [(i, h) for i in range(4) for h in range(2)]
 
+    def first_hop(way, q, crossing):
+        side = 1 - core if crossing else core
+        ends = (slant_up, slant_down) if crossing else (up, down)
+        return remote(
+            stage.at[chunks[q], :],
+            block(x_full, z, side, q * half, half),
+            gr_send.at[0, way, 0, q],
+            gr_recv.at[0, way, 0, q],
+            ends[way],
+        )
+
     @pl.when(place.away)
     def _():
-        for a, q in both:
-            swap(a, q).start()
+        for q in range(2):
+            for way in range(2):
+                first_hop(way, q, True).start()
+            swap(0, q).start()
+        for q in range(2):
+            swap(1, q).start()
         for i, h in weights:
             weight_swap(i, h).start()
 
     @pl.when(place.home)
     def _():
+        for q in range(2):
+            for way in range(2):
+                first_hop(way, q, False).start()
         for a, q in both:
             keep(a, q).start()
         for i, h in weights:
@@ -276,8 +305,9 @@
         def _():
             keep(a, q).wait()
 
-        for way in range(2):
-            gather(a, way, 0, q).start()
+        if a == 1:
+            for way in range(2):
+                gather(a, way, 0, q).start()
         own_pair(a, q).start()
 
     def advance(a, k, q):
@@ -498,36 +528,30 @@
     two(1, backward)
     z_step(0, 2, 0)
     one(3, backward)
-    z_step(0, 2, 1)
-
-    for j in range(4):
-        lanes = slice(j * 256, (j + 1) * 256)
-        for i in range(3):
-            backs[i * 256 : (i + 1) * 256, lanes] = dqkv[lanes, i * 256 : (i + 1) * 256].T
-        backs[768:1024, lanes] = att[lanes, :].T
-
-    def weight_grads(j):
-        cols = pl.ds(pl.multiple_of(j * 256, 256), 256)
-        for i in range(4):
+
+    def turn(i):
+        for j in range(4):
+            cut = slice(j * 256, (j + 1) * 256)
+            source = dqkv[cut, i * 256 : (i + 1) * 256] if i < 3 else att[cut, :]
+            backs[i * 256 : (i + 1) * 256, cut] = source.T
+
+    def weight_grads(s, q):
+        for i in (2 * s, 2 * s + 1):
             factor = backs[i * 256 : (i + 1) * 256, 0:1024]
-            total = nn(factor, (x_full if i < 3 else c_full)[:, cols]).astype(LOW)
+            total = nn(factor, (x_full if i < 3 else c_full)[:, columns(q)]).astype(LOW)
             for h in range(2):
                 spot = i * 160 + h * HEAD_DIM
-                g[spot : spot + HEAD_DIM, cols] = total[h * PAD : h * PAD + HEAD_DIM, :]
-
-    two(0, weight_grads)
-    z_step(0, 3, 0)
-    loop(8, lambda j: weight_grads(j + 2))
-
-    side_start, side_rows, subs, width = (0, 256), (256, 384), (64, 96), dim // 4
+                g[spot : spot + HEAD_DIM, columns(q)] = total[h * PAD : h * PAD + HEAD_DIM, :]
+
+    side_start, side_rows, subs, width = (0, 320), (320, 320), (80, 80), dim // 4
     firsts, seconds = (x, y), (y, x)
     neighbours = ((right, left), (north, south))
     lanes = (slice(0, 384), slice(384, 640))
     pieces = [(s, c) for c in range(2) for s in range(2)]
 
     def half_of(s, way, size):
-        count = size[s] // 2
-        return slice(way * count, (way + 1) * count)
+        count = (size[s] // 16 + 1) // 2 * 16
+        return slice(0, count) if way == 0 else slice(count, size[s])
 
     def columns(q):
         return pl.ds(pl.multiple_of(((q + 4) % 4) * width, 128), width)
@@ -536,7 +560,7 @@
         return g.at[pl.ds(side_start[s], side_rows[s]), columns(q)].at[:, lanes[c]]
 
     def sub_rows(s, q):
-        return pl.ds(pl.multiple_of(((q + 4) % 4) * subs[s], 32), subs[s])
+        return pl.ds(pl.multiple_of(((q + 4) % 4) * subs[s], 16), subs[s])
 
     def e_sub(s, q, c):
         return e_sum.at[s, sub_rows(s, q), lanes[c]]
@@ -589,7 +613,7 @@
             s_copy(s, way, 1, c).start()
 
     def work(s, row, col, c):
-        start = pl.multiple_of(side_start[s] + ((row + 4) % 4) * subs[s], 32)
+        start = pl.multiple_of(side_start[s] + ((row + 4) % 4) * subs[s], 16)
         return g_work.at[pl.ds(start, subs[s]), columns(col)].at[:, lanes[c]]
 
     def work_column(s, col, c):
@@ -622,6 +646,17 @@
         spot = work_column(0, source, c) if s == 0 else work(1, source, y, c)
         return remote(spot, spot, gh_send.at[s, i, c], gh_recv.at[s, i, c], pair)
 
+    relay_in = remote(
+        work_column(0, x, 1), work_column(0, x, 1), relay_send, relay_recv, left
+    )
+    relay_out = remote(
+        work_column(0, x + 1, 1),
+        work_column(0, x + 1, 1),
+        gh_send.at[0, 2, 1],
+        gh_recv.at[0, 2, 1],
+        left,
+    )
+
     def xa_start(s, c):
         @pl.when(place.away)
         def _():
@@ -630,7 +665,10 @@
 
         @pl.when(place.home)
         def _():
-            xa(s, 2, c).start()
+            if (s, c) == (0, 1):
+                relay_in.start()
+            else:
+                xa(s, 2, c).start()
 
     def handed(s, i, c):
         at = x if s == 0 else y
@@ -664,9 +702,32 @@
             ya(0, way, 1, c).wait_recv()
         xa_start(0, c)
 
-    for s, c in pieces:
-        for way in range(2):
-            f_copy(s, way, 0, c).start()
+    def f_start(s):
+        for c in range(2):
+            for way in range(2):
+                f_copy(s, way, 0, c).start()
+
+    turn(0)
+    turn(1)
+    weight_grads(0, x + 2)
+    f_start(0)
+    z_step(0, 2, 1)
+    turn(2)
+    turn(3)
+    weight_grads(1, y + 2)
+    f_start(1)
+    weight_grads(0, x + 1)
+    weight_grads(0, x - 1)
+    f_pass(0, 0)
+    f_pass(0, 1)
+    z_step(0, 3, 0)
+    weight_grads(1, y + 1)
+    weight_grads(1, y - 1)
+    f_pass(1, 0)
+    f_pass(1, 1)
+    z_step(0, 3, 1)
+    weight_grads(0, x)
+    weight_grads(1, y)
 
     def back_parts(j):
         here = pl.ds(pl.multiple_of(j * 256, 256), 256)
@@ -674,25 +735,20 @@
             cols = slice(i * 256, (i + 1) * 256)
             backs[here, cols] = nn(dqkv[here, :], wq[:, cols]).astype(LOW)
 
-    z_step(0, 3, 1)
     one(groups[0], back_parts)
     core_copies(1, (4,))
-    f_pass(0, 0)
-    f_pass(1, 0)
     one(groups[1], back_parts)
     z_step(1, 0, 0)
     z_step(1, 0, 1)
     one(groups[2], back_parts)
     core_copies(1, (3, -3, 2, -2))
-    f_pass(0, 1)
-    f_pass(1, 1)
+    f_final(0, 0)
     z_final(0, 0)
     z_step(1, 1, 0)
     one(groups[3], back_parts)
     core_copies(1, (1, -1, 0))
     z_final(0, 1)
     z_step(1, 1, 1)
-    f_final(0, 0)
     f_final(1, 0)
     z_step(1, 2, 0)
     s_pass(0, 0)
@@ -754,7 +810,7 @@
     def finish_gradient(i):
         here = pl.ds(pl.multiple_of(i * 16, 16), 16)
         xhat, rstd = standardize(tokens[here, :])
-        scaled = landed[1, here, :].astype(WIDE) * gain[...]
+        scaled = landed[1, here, :].astype(WIDE) * gain[...].reshape(1, dim)
         first = jnp.mean(scaled, axis=-1, keepdims=True)
         second = jnp.mean(scaled * xhat, axis=-1, keepdims=True)
         total = cot[here, :].astype(WIDE) + rstd * (scaled - first - xhat * second)
@@ -764,6 +820,11 @@
     loop(rows // 16, finish_output)
     z_final(1, 0)
     z_final(1, 1)
+    @pl.when(place.away)
+    def _():
+        relay_in.wait_recv()
+        relay_out.start()
+
     landing(1)
     loop(rows // 16, finish_gradient)
 
@@ -785,6 +846,7 @@
                 hand_pair(s, i, c).wait_recv()
             xa(s, 0, c).wait_send()
             xa(s, 1, c).wait_send()
+        relay_out.wait_send()
         for a, q in both:
             swap(a, q).wait_send()
             swap_back(a, q).wait_send()
@@ -797,7 +859,10 @@
             for i in range(4):
                 hand_pair(s, i, c).wait_send()
                 hand_out(s, i, c).wait()
-            xa(s, 2, c).wait_send()
+            if (s, c) == (0, 1):
+                relay_in.wait_send()
+            else:
+                xa(s, 2, c).wait_send()
         for way, k in both:
             for c in range(2):
                 ya(1, way, k, c).wait_send()
@@ -861,11 +926,11 @@
             low(2, rows, dim),
             low(2, rows, dim),
             low(sums, dim),
-            low(2, 384, quarter),
-            low(2, 2, 384, quarter),
-            low(2, 384, quarter),
-            low(2, 96, quarter),
-            low(2, 2, 96, quarter),
+            low(2, 320, quarter),
+            low(2, 2, 320, quarter),
+            low(2, 320, quarter),
+            low(2, 80, quarter),
+            low(2, 2, 80, quarter),
             low(sums, dim),
             dma((2, 2)),
             dma((2, 2)),
@@ -897,20 +962,77 @@
             dma((2, 4, 2)),
             dma((2, 4, 2)),
             dma((2, 4, 2)),
+            dma,
+            dma,
         ],
         compiler_params=pltpu.CompilerParams(
             collective_id=0, has_side_effects=True, vmem_limit_bytes=VMEM_BYTES
         ),
         name="attention_layer",
-    )(tokens, gain.reshape(1, dim), w_qkv, w_out, cotangent)
+    )(tokens, gain, w_qkv, w_out, cotangent)
+
+
+def widen_kernel(sums, out_in, ingrad_in, gq, go, out, ingrad, low_buf, wide_buf, in_sem, out_sem):
+    count, split = 80, gq.shape[0]
+    scale = 1.0 / lax.axis_size("dp")
+
+    def fetch(i):
+        spot = slice(i * count, (i + 1) * count)
+        return pltpu.make_async_copy(sums.at[spot, :], low_buf.at[spot, :], in_sem.at[i])
+
+    def store(i):
+        first = i * count
+        source = wide_buf.at[first : first + count, :]
+        ref, at = (gq, first) if first < split else (go, first - split)
+        return pltpu.make_async_copy(source, ref.at[at : at + count, :], out_sem.at[i])
+
+    steps = sums.shape[0] // count
+    for i in range(steps):
+        fetch(i).start()
+    out[...] = out_in[...]
+    ingrad[...] = ingrad_in[...]
+    for i in range(steps):
+        fetch(i).wait()
+
+        def widen(k):
+            here = pl.ds(pl.multiple_of(i * count + k * 16, 16), 16)
+            wide_buf[here, :] = low_buf[here, :].astype(WIDE) * scale
+
+        loop(count // 16, widen)
+        store(i).start()
+    for i in range(steps):
+        store(i).wait()
+
+
+def widen_sums(sums, output, input_gradient, width):
+    total, dim = sums.shape
+    vmem = pl.BlockSpec(memory_space=pltpu.VMEM)
+    any_space = pl.BlockSpec(memory_space=pl.ANY)
+    return pl.pallas_call(
+        widen_kernel,
+        out_shape=(
+            jax.ShapeDtypeStruct((3 * width, dim), WIDE),
+            jax.ShapeDtypeStruct((total - 3 * width, dim), WIDE),
+            jax.ShapeDtypeStruct(output.shape, LOW),
+            jax.ShapeDtypeStruct(output.shape, LOW),
+        ),
+        in_specs=[any_space, vmem, vmem],
+        out_specs=(any_space, any_space, vmem, vmem),
+        scratch_shapes=[
+            pltpu.VMEM((total, dim), LOW),
+            pltpu.VMEM((total, dim), WIDE),
+            pltpu.SemaphoreType.DMA((8,)),
+            pltpu.SemaphoreType.DMA((8,)),
+        ],
+        compiler_params=pltpu.CompilerParams(vmem_limit_bytes=VMEM_BYTES),
+        name="widen_sums",
+    )(sums, output, input_gradient)
 
 
 def per_device(tokens, gain, w_qkv, w_out, cotangent):
     width = w_out.shape[0]
     output, input_gradient, sums = run_layer(tokens, gain, w_qkv, w_out, cotangent)
-    replicas = lax.axis_size("dp")
-    grad_qkv = sums[: 3 * width].astype(jnp.float32) / replicas
-    grad_out = sums[3 * width :].astype(jnp.float32) / replicas
+    grad_qkv, grad_out, output, input_gradient = widen_sums(sums, output, input_gradient, width)
     return (output, input_gradient, grad_qkv.reshape(w_qkv.shape), grad_out)
 
 

time: 153 us -> 145 us (0.948)
  other arithmetic: 7.14 us -> 0 us
  local copies, waits for them, and re-layouts: 2.77 us -> 0 us
  Pallas kernels: 142 us -> 144 us
    div x2 -> x0, other arithmetic: 7.14 us -> none  [the longest x1 4.66 us: per_device(): grad_qkv = sums[:3 * width].astype(jnp.float32) / replicas]
    pallas_call x0 -> x1, Pallas kernels: none -> 5.88 us  [widen_sums(): pl.pallas_call(widen_kernel, out_shape=(jax.ShapeDtypeStruct((3 * width,...]
    pallas_call x1, Pallas kernels: 142 us -> 138 us  [run_layer(): pl.pallas_call(layer_kernel, out_shape=(jax.ShapeDtypeStruct((rows, dim),...]
where the time goes in v4:
time: 145 us
  Pallas kernels  144 us (99%)
    pallas_call x1, Pallas kernels, run_layer(): pl.pallas_call(layer_kernel, out_shape=(jax.ShapeDtypeStruct((rows, dim),...  138 us
    pallas_call x1, Pallas kernels, widen_sums(): pl.pallas_call(widen_kernel, out_shape=(jax.ShapeDtypeStruct((3 * width,...  5.88 us

profile of v4, /device:TPU:1, one launch (start us, length us, event | category | flops | bytes accessed | tf_op | source)
XLA Modules:
  0.0 144.7 jit_solution(1739829195534883956)
XLA Ops:
  0.6 138.0 %attention_layer.1 = (bf16[64,2560]{1,0:T(8,128)(2,1)}, bf16[64,2560]{1,0:T(8,128)(2,1)}, bf16[640,2560]{1,0:T(8,128)(2,1)}) custom-call(bf16[64,2560]{1,0:T(8,128)(2,1)} %tokens.1, f32[2560]{0:T(1024)} %gain.1, bf16[3,160,2560]{2,1,0:T(8,128)(2,1)} %wq_ref.1, bf16[160,2560]{1,0:T(8,128)(2,1)} %wo_ref.1, bf16[64,2560]{1,0:T(8,128)(2,1)} %cot.1), custom_call_target="tpu_custom_call" | custom-call | tf_op jit(solution)/shard_map/attention_layer/pallas_call | solution.py:899
  138.6 5.9 %widen_sums.1 = (f32[480,2560]{1,0:T(8,128)}, f32[160,2560]{1,0:T(8,128)}, bf16[64,2560]{1,0:T(8,128)(2,1)}, bf16[64,2560]{1,0:T(8,128)(2,1)}) custom-call(bf16[640,2560]{1,0:T(8,128)(2,1)} %get-tuple-element.11.sums, bf16[64,2560]{1,0:T(8,128)(2,1)} %get-tuple-element.12.out_in, bf16[64,2560]{1,0:T(8,128)(2,1)} %get-tuple-element.13.ingrad_in), custom_call_target="tpu_custom_call" | custom-call | tf_op jit(solution)/shard_map/widen_sums/pallas_call | solution.py:1011

commit v5 on v4

--- a/solution.py
+++ b/solution.py
@@ -205,11 +205,11 @@
         wo[i * PAD + HEAD_DIM : (i + 1) * PAD, :] = jnp.zeros((PAD - HEAD_DIM, dim), LOW)
 
     def norm_rows(i):
-        here = pl.ds(pl.multiple_of(i * 16, 16), 16)
+        here = pl.ds(pl.multiple_of(i * 32, 32), 32)
         xhat, _ = standardize(tokens[here, :])
         stage[here, :] = (xhat * gain[...].reshape(1, dim)).astype(LOW)
 
-    loop(rows // 16, norm_rows)
+    loop(rows // 32, norm_rows)
     met(len(others))
 
     def block(full, owner, side, first=0, count=rows):
@@ -320,11 +320,13 @@
 
     hop_list = [(way, k, q) for k in range(4) for q in range(2) for way in range(2) if k < hops(way, q)]
 
-    def gathered(a):
-        for q in range(2):
-            own_pair(a, q).wait_recv()
+    def gathered(a, hop_counts):
+        if 0 in hop_counts:
+            for q in range(2):
+                own_pair(a, q).wait_recv()
         for way, k, q in hop_list:
-            to_pair(a, way, k, q).wait_recv()
+            if k in hop_counts:
+                to_pair(a, way, k, q).wait_recv()
 
     for q in range(2):
         begin(0, q)
@@ -346,7 +348,7 @@
         for i, h in weights:
             weight_keep(i, h).wait()
 
-    gathered(0)
+    gathered(0, range(4))
 
     def project(j):
         here = pl.ds(pl.multiple_of(j * 256, 256), 256)
@@ -489,13 +491,17 @@
     z_step(0, 0, 1)
     one(groups[3], out_parts)
     core_copies(0, (1, -1, 0))
-    advance(1, 3, 0)
-    advance(1, 3, 1)
-    gathered(1)
-
     def project_back(j):
         here = pl.ds(pl.multiple_of(j * 256, 256), 256)
         datt[here, :] = nt(c_full[here, :], wo[...]).astype(LOW)
+
+    gathered(1, range(3))
+    for group in (groups[3], groups[1], groups[2]):
+        one(group, project_back)
+    advance(1, 3, 0)
+    advance(1, 3, 1)
+    gathered(1, (3,))
+    one(groups[0], project_back)
 
     def backward(u):
         r0, c0 = spots(u)
@@ -521,7 +527,6 @@
         dqkv[pl.ds(r0, LEN), pl.ds(c0 + 256, PAD)] = dk_sum[...].astype(LOW)
         dqkv[pl.ds(r0, LEN), pl.ds(c0 + 512, PAD)] = dv_sum[...].astype(LOW)
 
-    loop(4, project_back)
     z_step(0, 1, 0)
     one(0, backward)
     z_step(0, 1, 1)
@@ -808,7 +813,7 @@
         out_ref[here, :] = (tokens[here, :].astype(WIDE) + landed[0, here, :].astype(WIDE)).astype(LOW)
 
     def finish_gradient(i):
-        here = pl.ds(pl.multiple_of(i * 16, 16), 16)
+        here = pl.ds(pl.multiple_of(i * 32, 32), 32)
         xhat, rstd = standardize(tokens[here, :])
         scaled = landed[1, here, :].astype(WIDE) * gain[...].reshape(1, dim)
         first = jnp.mean(scaled, axis=-1, keepdims=True)
@@ -826,7 +831,7 @@
         relay_out.start()
 
     landing(1)
-    loop(rows // 16, finish_gradient)
+    loop(rows // 32, finish_gradient)
 
     @pl.when(place.home)
     def _():

time: 145 us -> 144 us (level)
  no operation moved by 1% of the time
where the time goes in v5:
time: 144 us
  Pallas kernels  143 us (99%)
    pallas_call x1, Pallas kernels, run_layer(): pl.pallas_call(layer_kernel, out_shape=(jax.ShapeDtypeStruct((rows, dim),...  137 us
    pallas_call x1, Pallas kernels, widen_sums(): pl.pallas_call(widen_kernel, out_shape=(jax.ShapeDtypeStruct((3 * width,...  5.88 us

profile of v5, /device:TPU:1, one launch (start us, length us, event | category | flops | bytes accessed | tf_op | source)
XLA Modules:
  0.0 143.7 jit_solution(5807311468858251892)
XLA Ops:
  0.6 137.0 %attention_layer.1 = (bf16[64,2560]{1,0:T(8,128)(2,1)}, bf16[64,2560]{1,0:T(8,128)(2,1)}, bf16[640,2560]{1,0:T(8,128)(2,1)}) custom-call(bf16[64,2560]{1,0:T(8,128)(2,1)} %tokens.1, f32[2560]{0:T(1024)} %gain.1, bf16[3,160,2560]{2,1,0:T(8,128)(2,1)} %wq_ref.1, bf16[160,2560]{1,0:T(8,128)(2,1)} %wo_ref.1, bf16[64,2560]{1,0:T(8,128)(2,1)} %cot.1), custom_call_target="tpu_custom_call" | custom-call | tf_op jit(solution)/shard_map/attention_layer/pallas_call | solution.py:904
  137.6 5.9 %widen_sums.1 = (f32[480,2560]{1,0:T(8,128)}, f32[160,2560]{1,0:T(8,128)}, bf16[64,2560]{1,0:T(8,128)(2,1)}, bf16[64,2560]{1,0:T(8,128)(2,1)}) custom-call(bf16[640,2560]{1,0:T(8,128)(2,1)} %get-tuple-element.11.sums, bf16[64,2560]{1,0:T(8,128)(2,1)} %get-tuple-element.12.out_in, bf16[64,2560]{1,0:T(8,128)(2,1)} %get-tuple-element.13.ingrad_in), custom_call_target="tpu_custom_call" | custom-call | tf_op jit(solution)/shard_map/widen_sums/pallas_call | solution.py:1016
